TPU v7x, 256 devices: a whole 4x4x8 slice. The times are simulated.
256 devices in a mesh: dp: 2 (over z_lo), row: 4 (over y), col: 32 (over z_hi, x, core).
Axes of the slice: x: 4, y: 4, z: 8 (z_hi: 4, z_lo: 2; z = z_hi * 2 + z_lo), core: 2. Of those that a mesh axis runs over, the one named last changes fastest.
Arguments:
- states: bfloat16 [2, 1024, 5120], P('dp', 'row', 'col'), may hold values from -80 to 80
- cotangent: bfloat16 [2, 1024, 5120], P('dp', 'row', 'col'), may hold values from -6 to 6
- shift_mod: float32 [2, 5120], P('dp', 'col'), may hold values from -5 to 5
- scale_mod: float32 [2, 5120], P('dp', 'col'), may hold values from -2.5 to 2.5
- gate_mod: float32 [2, 5120], P('dp', 'col'), may hold values from -5 to 5
- first_weight: bfloat16 [5120, 13824], P('row', 'col'), may hold values from -0.15625 to 0.15625
- second_weight: bfloat16 [5120, 13824], P('row', 'col'), may hold values from -0.09375 to 0.09375
Outputs:
- grad_states: float32 [2, 1024, 5120], P('dp', 'row', 'col')
- grad_first: float32 [5120, 13824], P('row', 'col')
- grad_second: float32 [5120, 13824], P('row', 'col')
- grad_shift: float32 [2, 5120], P('dp', 'col')
- grad_scale: float32 [2, 5120], P('dp', 'col')
- grad_gate: float32 [2, 5120], P('dp', 'col')
All inputs are finite; a program needn't handle non-finite values.
Results may differ from a plain program's by a relative error of at most 0.039.
Values may be sent and summed in bfloat16 or wider, within the bound.
No kernel may reach another device: no remote copies, remote signals or barrier semaphores. Data moves between devices by JAX's collectives and lax.ppermute only.
A program may use at most 128 MiB of HBM per device.

v0:
```python
import functools
import math

import jax
import jax.numpy as jnp
from jax import lax
from jax.experimental import pallas as pl
from jax.experimental.pallas import tpu as pltpu
from jax.sharding import PartitionSpec as P

D = 5120
FF = 13824
ROWS = 4
COLS = 32
INNER = 8
CHANNELS = D // COLS
UNITS = FF // COLS
TOK = 256
SLICE = D // ROWS
TOKENS = ROWS * TOK
EXTRA = 16
CHUNK = 256

bf16, f32 = jnp.bfloat16, jnp.float32

eps = 1e-06
tanh_factor = 0.7978845608028654
cubic_term = 0.044715
token_scale = 1.0 / math.sqrt(ROWS * TOK)
weight_scale = 1.0 / math.sqrt(2 * ROWS * TOK)
across_tokens = (((1,), (1,)), ((), ()))


def gelu_pair(values):
    squares = values * values
    inner = jnp.tanh(tanh_factor * (values + cubic_term * squares * values))
    half = 0.5 * (1.0 + inner)
    slope = half + 0.5 * values * (1.0 - inner * inner) * tanh_factor * (
        1.0 + 3.0 * cubic_term * squares
    )
    return values * half, slope


def turn(value, offset):
    return lax.rem(value + offset + 8, 4)


def spread_rows(values, shift):
    pairs = [
        (a * COLS + b * INNER + i, b * COLS + ((a + shift) % 4) * INNER + i)
        for a in range(4)
        for b in range(4)
        for i in range(INNER)
    ]
    return lax.ppermute(values, ("row", "col"), pairs)


def along_high(values, shift):
    pairs = [(h * 8 + i, ((h + shift) % 4) * 8 + i) for h in range(4) for i in range(INNER)]
    return lax.ppermute(values, "col", pairs)


def along_x(values, shift):
    pairs = [
        (h * 8 + x * 2 + k, h * 8 + ((x + shift) % 4) * 2 + k)
        for h in range(4)
        for x in range(4)
        for k in range(2)
    ]
    return lax.ppermute(values, "col", pairs)


def across(values):
    return lax.ppermute(values, "col", [(c, c ^ 1) for c in range(COLS)])


def along_row(values, shift):
    return lax.ppermute(values, "row", [(a, (a + shift) % 4) for a in range(4)])


def all_rows(values):
    return [values] + [along_row(values, q) for q in (1, 2, 3)]


def to_rows(values):
    return [values[0]] + [along_row(values[q], q) for q in (1, 2, 3)]


def swap_clips(values):
    return lax.ppermute(values, "dp", [(0, 1), (1, 0)])


def both_cores(pos, lines):
    shape = shaped((2 * lines[0].shape[0], TOK))
    packs = whole(pair_kernel, [shape, shape])(pos, *lines)
    return list(lines) + [across(pack) for pack in packs]


def after(values, other):
    return lax.optimization_barrier((values, other))[0]


cheap = pl.CostEstimate(flops=1024, bytes_accessed=1024, transcendentals=0)
some = pl.CostEstimate(flops=1024, bytes_accessed=8000000, transcendentals=0)
limit = pltpu.CompilerParams(vmem_limit_bytes=16 * 1024 * 1024)


def call(kernel, grid, in_specs, out_specs, out_shape, scratch=()):
    return pl.pallas_call(
        kernel,
        grid_spec=pltpu.PrefetchScalarGridSpec(
            num_scalar_prefetch=1,
            grid=grid,
            in_specs=in_specs,
            out_specs=out_specs,
            scratch_shapes=list(scratch),
        ),
        out_shape=out_shape,
        compiler_params=limit,
        cost_estimate=cheap,
    )


def whole(kernel, out_shape, scratch=(), cost=cheap):
    vmem = pl.BlockSpec(memory_space=pltpu.VMEM)

    def run(pos, *args):
        return pl.pallas_call(
            kernel,
            in_specs=[pl.BlockSpec(memory_space=pltpu.SMEM)] + [vmem] * len(args),
            out_specs=[vmem] * len(out_shape),
            out_shape=out_shape,
            scratch_shapes=list(scratch),
            compiler_params=limit,
            cost_estimate=cost,
        )(pos, *args)

    return run


def full(shape):
    return pl.BlockSpec(shape, lambda i, pos: (0,) * len(shape))


def shaped(shape, kind=bf16):
    return jax.ShapeDtypeStruct(shape, kind)


def place_of(pos, token):
    return turn(pos[1] - token, -1)


def channel_block(pos, q, flip):
    core = pos[3] if flip == 0 else 1 - pos[3]
    return turn(pos[2], -q) * 2 + core


def parts_of(values, count):
    parts = []
    for _ in range(count):
        parts.append(values.astype(bf16).astype(f32))
        values = values - parts[-1]
    return parts


def packed(values):
    return jnp.concatenate(parts_of(values, 2), 0).astype(bf16)


def unpacked(rows):
    wide = rows.astype(f32)
    return wide[0:8] + wide[8:16]


def pack_kernel(pos, plain, mods, out):
    line = lax.broadcasted_iota(jnp.int32, (3, CHANNELS), 0)
    values = mods[...] + jnp.where(line == 1, 1.0, 0.0)
    rows = parts_of(values, 3) + [jnp.zeros((EXTRA - 9, CHANNELS), f32)]
    out[: 2 * CHANNELS] = plain[...]
    out[2 * CHANNELS :] = jnp.zeros((EXTRA, TOK), bf16)
    out[2 * CHANNELS :, :CHANNELS] = jnp.concatenate(rows, 0).astype(bf16)


def pair_kernel(pos, l0, l1, l2, l3, first, second):
    rows = l0.shape[0]
    first[:rows], first[rows:] = l0[...], l1[...]
    second[:rows], second[rows:] = l2[...], l3[...]


def block_of(blocks, q, flip, at, size):
    if flip == 0:
        return blocks[q][pl.ds(at, size), :]
    rows = blocks[0].shape[0]
    return blocks[4 + q // 2][pl.ds(at + (q % 2) * rows, size), :]


def sort_kernel(pos, b0, b1, b2, b3, x, cot):
    for at, ref in enumerate((b0, b1, b2, b3)):
        rows = slice(at * CHANNELS, (at + 1) * CHANNELS)
        x[rows] = ref[:CHANNELS]
        cot[rows] = ref[CHANNELS : 2 * CHANNELS]
    x[4 * CHANNELS :] = b3[2 * CHANNELS :]


def turned_kernel(pos, w1, out):
    out[...] = w1[...].T


def mods_kernel(pos, *refs):
    blocks, w1, mods_column, mods_row, through_out = refs[:6], refs[6], refs[7], refs[8], refs[9]
    for q in range(4):
        for flip in range(2):
            rows = block_of(blocks, q, flip, 4 * CHANNELS, EXTRA).astype(f32)
            values = jnp.concatenate([rows[0:3] + rows[3:6] + rows[6:9], rows[9:14]], 0)
            mods_column[channel_block(pos, q, flip)] = values.T[:CHANNELS]
    values = mods_column[...].reshape(SLICE, 8).T
    mods_row[...] = values
    rows = jnp.concatenate(parts_of(values, 3) + [jnp.zeros_like(values)], 0).astype(bf16)
    through = lax.dot_general(rows, w1[...], across_tokens, preferred_element_type=f32)
    through = through[0:8] + through[8:16] + through[16:24]
    through_out[...] = jnp.zeros((8, TOK), f32)
    for at, line in ((0, through[1:2]), (2, through[0:1])):
        through_out[at : at + 1] = line[:, :TOK]
        through_out[at + 1 : at + 2, : UNITS - TOK] = line[:, TOK:]


def first_kernel(shift, pos, *refs):
    blocks, mods, through, w1 = refs[:6], refs[6], refs[7], refs[8]
    out, offset_out, mean_out, offsets = refs[9:]
    place = place_of(pos, turn(pos[0], shift))
    at = pl.multiple_of(place * CHANNELS, 32)
    total = 0.0
    for q in range(4):
        for flip in range(2):
            block = block_of(blocks, q, flip, at, CHANNELS).astype(f32)
            total = total + jnp.sum(block, 0, keepdims=True)
    mean = total / SLICE
    square = 0.0
    for q in range(4):
        for flip in range(2):
            j = channel_block(pos, q, flip)
            offset = block_of(blocks, q, flip, at, CHANNELS).astype(f32) - mean
            square = square + jnp.sum(offset * offset, 0, keepdims=True)
            offsets[j] = (offset * mods[j][:, 1:2]).astype(bf16)
            rows = pl.ds(pl.multiple_of(j * CHANNELS, 32), CHANNELS)
            offset_out[rows, :] = offset.astype(bf16)
    mean_out[...] = mean
    out[:UNITS] = jnp.dot(
        w1[...], offsets[...].reshape(SLICE, TOK), preferred_element_type=f32
    ).astype(bf16)
    four = jnp.concatenate([mean, square, through[0:2]], 0)
    extra = parts_of(four, 3) + parts_of(through[2:4], 2)
    out[UNITS:] = jnp.concatenate(extra, 0).astype(bf16)


def hidden_kernel(pos, p0, p1, p2, p3, hidden_out, slope_out, rest_out, factor_out, stats_out):
    parts = (p0, p1, p2, p3)
    extras = [ref[UNITS:].astype(f32) for ref in parts]
    fours = [e[0:4] + e[4:8] + e[8:12] for e in extras]
    shifts = sum(e[12:14] + e[14:16] for e in extras)
    centre = 0.25 * (fours[0][0:1] + fours[1][0:1] + fours[2][0:1] + fours[3][0:1])
    spread = 0.0
    for four in fours:
        spread = spread + four[1:2] + SLICE * (four[0:1] - centre) ** 2
    inverse = lax.rsqrt(spread / D + eps)
    stats = jnp.concatenate([centre, inverse], 0)
    stats_out[...] = stats
    hidden_out[UNITS:] = jnp.concatenate(
        parts_of(stats, 3) + [jnp.zeros((EXTRA - 6, TOK), f32)], 0
    ).astype(bf16)
    columns = jnp.concatenate([four[2:4] for four in fours] + [shifts] * 4, 0).T
    for half, at in ((0, slice(0, TOK)), (1, slice(TOK, UNITS))):
        size = at.stop - at.start
        rest, total = 0.0, 0.0
        for i, ref in enumerate(parts):
            factor = columns[:size, 2 * i + half : 2 * i + half + 1]
            total = total + factor
            rest = rest + (ref[at].astype(f32) + factor * (fours[i][0:1] - centre))
        rest = rest * inverse
        hidden, slope = gelu_pair(rest + columns[:size, 8 + half : 9 + half])
        hidden_out[at] = hidden.astype(bf16)
        slope_out[at] = slope
        rest_out[at] = rest
        factor_out[at] = total


def second_kernel(pos, *refs):
    blocks, mods, w2 = refs[:6], refs[6], refs[7]
    sums, cot_out, scaled = refs[8:12], refs[12], refs[13]
    for shift, out in enumerate(sums):
        token = turn(pos[0], shift)
        at = pl.multiple_of(place_of(pos, token) * CHANNELS, 32)
        lanes = pl.ds(pl.multiple_of(token * TOK, TOK), TOK)
        for q in range(4):
            for flip in range(2):
                j = channel_block(pos, q, flip)
                block = block_of(blocks, q, flip, at, CHANNELS)
                rows = pl.ds(pl.multiple_of(j * CHANNELS, 32), CHANNELS)
                cot_out[rows, lanes] = block
                scaled[shift, rows, :] = (block.astype(f32) * mods[j][:, 2:3]).astype(bf16)
        out[...] = jnp.dot(w2[...], scaled[shift], preferred_element_type=f32).astype(bf16)


def grad_kernel(pos, own, one, two, three, slope, rest, factor, out):
    grad = own[...].astype(f32) + one[...].astype(f32)
    grad = grad + (two[...].astype(f32) + three[...].astype(f32))
    grad = (grad * slope[...]).astype(bf16)
    out[:UNITS] = grad
    wide = grad.astype(f32)
    first = jnp.sum(wide * factor[...], 0, keepdims=True)
    second = jnp.sum(wide * rest[...], 0, keepdims=True)
    line = lax.broadcasted_iota(jnp.int32, (8, TOK), 0)
    out[UNITS:] = packed(jnp.where(line == 3, first, jnp.where(line == 4, second, 0.0)))


def collect(pos, refs, store):
    for q, ref in enumerate(refs):
        at = pl.multiple_of(turn(pos[0], -q) * TOK, TOK)
        store[:, pl.ds(at, TOK)] = ref[:UNITS]


def second_weight_kernel(pos, b0, b1, b2, b3, cot, mods, w2, send, sums, store):
    collect(pos, (b0, b1, b2, b3), store)
    line = lax.broadcasted_iota(jnp.int32, (8, CHUNK), 0)
    for at in range(0, SLICE, CHUNK):
        part = slice(at, at + CHUNK)
        raw = lax.dot_general(
            store[...], cot[part, :], across_tokens, preferred_element_type=f32
        )
        total = jnp.sum(w2[:, part].astype(f32) * raw, 0, keepdims=True)
        sums[part, :] = jnp.where(line == 2, total, 0.0).T
        send[:, part] = (raw * (mods[2:3, part] * weight_scale)).astype(bf16)


def first_weight_kernel(pos, *refs):
    grads, hiddens, offsets, means = refs[:4], refs[4:8], refs[8:12], refs[12:16]
    mods, w1, send, sums, store, others = refs[16:]
    total, lift = 0.0, 0.0
    for q in range(4):
        at = (4 - q) % 4
        extra = hiddens[q][UNITS:].astype(f32)
        stats = extra[0:2] + extra[2:4] + extra[4:6]
        grad = grads[q][:UNITS].astype(f32)
        total = total + jnp.sum(grad, 1, keepdims=True)
        grad = grad * stats[1:2]
        lift = lift + jnp.sum(grad * (means[at][...] - stats[0:1]), 1, keepdims=True)
        lanes = slice(at * TOK, (at + 1) * TOK)
        store[:, lanes] = grad.astype(bf16)
        others[:, lanes] = offsets[at][...]
    line = lax.broadcasted_iota(jnp.int32, (8, CHUNK), 0)
    for at in range(0, SLICE, CHUNK):
        part = slice(at, at + CHUNK)
        raw = lift + lax.dot_general(
            store[...], others[part, :], across_tokens, preferred_element_type=f32
        )
        weight = w1[:, part].astype(f32)
        shift = jnp.sum(weight * total, 0, keepdims=True)
        scale = jnp.sum(weight * raw, 0, keepdims=True)
        sums[part, :] = jnp.where(line == 0, shift, jnp.where(line == 1, scale, 0.0)).T
        grad = (raw * mods[1:2, part] + total * mods[0:1, part]) * weight_scale
        send[:, part] = grad.astype(bf16)


def mod_kernel(pos, g0, g1, g2, g3, w1, sums_one, sums_two, *rest):
    keeps, sends, store, line = rest[:4], rest[4:8], rest[8], rest[9]
    grads = (g0, g1, g2, g3)
    collect(pos, grads, store)
    line[...] = jnp.zeros((8, TOK), f32)
    smalls = [unpacked(ref[UNITS:]) for ref in grads]
    for core, outs in ((pos[3], keeps), (1 - pos[3], sends)):
        for p, out in enumerate(outs):
            j = turn(pos[2], p) * 2 + core
            rows = pl.ds(pl.multiple_of(j * CHANNELS, 32), CHANNELS)
            product = jnp.dot(w1[rows, :], store[...], preferred_element_type=f32).astype(bf16)
            for token in range(4):
                out[turn(token, -pos[0]), :CHANNELS] = product[
                    :, token * TOK : (token + 1) * TOK
                ]
            line[:, :CHANNELS] = (sums_one[j] + sums_two[j]).T
            for q, small in enumerate(smalls):
                out[(4 - q) % 4, CHANNELS:] = packed(small + line[...])


def add_up(out, parts):
    total = parts[0][:CHANNELS].astype(f32)
    small = unpacked(parts[0][CHANNELS:])
    for part in parts[1:]:
        total = total + part[:CHANNELS].astype(f32)
        small = small + unpacked(part[CHANNELS:])
    out[:CHANNELS] = total.astype(bf16)
    out[CHANNELS:] = packed(small)


def core_kernel(pos, *refs):
    for keep, other, out in zip(refs[:4], refs[4:8], refs[8:]):
        for s in range(4):
            add_up(out.at[s], [keep.at[s], other.at[s]])


def plane_kernel(pos, own, one, two, three, o0, o1, o2, o3):
    for s, out in enumerate((o0, o1, o2, o3)):
        add_up(out, [ref.at[s] for ref in (own, one, two, three)])


def route_kernel(pos, a0, a1, a2, a3, o0, o1, o2, o3, held):
    for q, ref in enumerate((a0, a1, a2, a3)):
        held[turn(pos[0], -q)] = ref[...]
    for p, out in enumerate((o0, o1, o2, o3)):
        out[...] = held[turn(pos[1], p)]


def states_kernel(pos, a0, a1, a2, a3, x, cot, stats, scale, out, *mods_out):
    centre, inverse = stats[0:1], stats[1:2]
    grad_mod, small = 0.0, 0.0
    for ref in (a0, a1, a2, a3):
        grad_mod = grad_mod + ref[:CHANNELS].astype(f32)
        small = small + unpacked(ref[CHANNELS:])
    normed = (x[...].astype(f32) - centre) * inverse
    grad_normed = grad_mod * (1.0 + scale[...])
    out[...] = cot[...].astype(f32) + inverse * (
        grad_normed - small[3:4] / D - normed * (small[4:5] / D)
    )
    for at, ref in enumerate(mods_out):
        ref[...] = small[at : at + 1, :CHANNELS] * token_scale


def clips_kernel(pos, own, other, out):
    out[...] = own[...].astype(f32) + other[...].astype(f32)


def on_device(states, cotangent, shift_mod, scale_mod, gate_mod, first_weight, second_weight):
    row, col = lax.axis_index("row"), lax.axis_index("col")
    high, x, core = col // INNER, lax.rem(col, INNER) // 2, lax.rem(col, 2)
    pos = jnp.stack([row, high, x, core]).astype(jnp.int32)
    weight_one, weight_two = first_weight.T, second_weight.T
    own_x, own_c = states[0].T, cotangent[0].T

    own = (CHANNELS, TOK)
    piece = (CHANNELS + EXTRA, TOK)
    units = (UNITS, TOK)
    wide_units = (UNITS + EXTRA, TOK)
    stage = pltpu.VMEM((INNER, CHANNELS, TOK), bf16)

    pair = (2 * CHANNELS, TOK)
    wide_pair = (2 * CHANNELS + EXTRA, TOK)
    plain = jnp.concatenate([own_x, own_c], 0)
    (with_mods,) = whole(pack_kernel, [shaped(wide_pair)])(
        pos, plain, jnp.concatenate([shift_mod, scale_mod, gate_mod], 0)
    )
    x_planes, c_planes = whole(
        sort_kernel,
        [shaped((4 * CHANNELS + EXTRA, TOK)), shaped((4 * CHANNELS, TOK))],
    )(pos, *[spread_rows(plain, s) for s in (1, 2, 3)], spread_rows(with_mods, 0))
    x_lines = [x_planes] + [along_x(x_planes, q) for q in (1, 2, 3)]
    (first_turned,) = whole(turned_kernel, [shaped((SLICE, UNITS))])(pos, weight_one)
    x_blocks = both_cores(pos, after(x_lines, first_turned))
    c_lines = [c_planes] + [along_x(c_planes, q) for q in (1, 2, 3)]

    mods_column, mods_row, through = whole(
        mods_kernel,
        [
            shaped((INNER, CHANNELS, 8), f32),
            shaped((8, SLICE), f32),
            shaped((8, TOK), f32),
        ],
    )(pos, *x_blocks, weight_one)

    pre_sums, offsets, means = [None] * 4, [None] * 4, [None] * 4
    blocks = x_blocks
    for shift in (1, 3, 2, 0):
        pre_sums[shift], offsets[shift], means[shift] = whole(
            functools.partial(first_kernel, shift),
            [shaped(wide_units), shaped((SLICE, TOK)), shaped((1, TOK), f32)],
            [stage],
            some,
        )(pos, *blocks, mods_column, through, weight_one)
        blocks = after(blocks, pre_sums[shift])
    pre_sums = to_rows(pre_sums)
    hidden, slope, rest, factor, stats = whole(
        hidden_kernel,
        [
            shaped(wide_units),
            shaped(units, f32),
            shaped(units, f32),
            shaped((UNITS, 1), f32),
            shaped((2, TOK), f32),
        ],
    )(pos, *pre_sums)
    c_blocks = both_cores(pos, after(c_lines, pre_sums))
    *grad_sums, cot = whole(
        second_kernel,
        [shaped(units)] * 4 + [shaped((SLICE, TOKENS))],
        [pltpu.VMEM((4, SLICE, TOK), bf16)],
    )(pos, *c_blocks, mods_column, weight_two)
    hidden = all_rows(hidden)

    weights = pl.BlockSpec((UNITS, CHUNK), lambda i, pos: (0, i))
    scratch = [pltpu.VMEM((UNITS, TOKENS), bf16)]

    weight_shapes = [shaped((UNITS, SLICE)), shaped((SLICE, 8), f32)]
    own_second, sums_second = whole(second_weight_kernel, weight_shapes, scratch)(
        pos, *hidden, cot, mods_row, weight_two
    )
    other_second = swap_clips(own_second)
    grad_sums = to_rows(after(grad_sums, hidden[2]))
    (grad_pre,) = whole(grad_kernel, [shaped(wide_units)])(
        pos, *grad_sums, slope, rest, factor
    )
    grad_pre = all_rows(grad_pre)
    own_first, sums_first = whole(
        first_weight_kernel, weight_shapes, scratch + [pltpu.VMEM((SLICE, TOKENS), bf16)]
    )(pos, *grad_pre, *hidden, *offsets, *means, mods_row, weight_one)
    other_first = swap_clips(own_first)

    quarter = (4,) + piece
    terms = whole(
        mod_kernel, [shaped(quarter)] * 8, scratch + [pltpu.VMEM((8, TOK), f32)]
    )(
        pos,
        *grad_pre,
        first_turned,
        sums_first.reshape(INNER, CHANNELS, 8),
        sums_second.reshape(INNER, CHANNELS, 8),
    )
    lines = whole(core_kernel, [shaped(quarter)] * 4)(
        pos, *terms[:4], *after([across(term) for term in terms[4:]], other_second)
    )
    def clips_call(own, other):
        return call(
            clips_kernel,
            (SLICE // CHUNK,),
            [weights, weights],
            weights,
            shaped((UNITS, SLICE), f32),
        )(pos, own, other)

    grad_second = clips_call(own_second, other_second)
    planes = whole(plane_kernel, [shaped(piece)] * 4)(
        pos, lines[0], *after([along_x(lines[p], p) for p in (1, 2, 3)], grad_second)
    )
    planes = to_rows(planes)
    pieces = whole(route_kernel, [shaped(piece)] * 4, [pltpu.VMEM((4,) + piece, bf16)])(
        pos, *planes
    )
    pieces = [pieces[0]] + [along_high(pieces[p], p) for p in (1, 2, 3)]

    grad_first = clips_call(own_first, other_first)
    grad_states, grad_shift, grad_scale, grad_gate = whole(
        states_kernel, [shaped(own, f32)] + [shaped((1, CHANNELS), f32)] * 3
    )(pos, *after(pieces, grad_first), own_x, own_c, stats, scale_mod.T)
    return (
        grad_states.T[None],
        grad_first.T,
        grad_second.T,
        grad_shift,
        grad_scale,
        grad_gate,
    )


def solution(mesh):
    return jax.shard_map(
        on_device,
        mesh=mesh,
        in_specs=(
            P("dp", "row", "col"),
            P("dp", "row", "col"),
            P("dp", "col"),
            P("dp", "col"),
            P("dp", "col"),
            P("row", "col"),
            P("row", "col"),
        ),
        out_specs=(
            P("dp", "row", "col"),
            P("row", "col"),
            P("row", "col"),
            P("dp", "col"),
            P("dp", "col"),
            P("dp", "col"),
        ),
        check_vma=False,
    )
```

profile of v0, /device:TPU:6, one launch (start us, length us, event | category | flops | bytes accessed | tf_op | source)
XLA Modules:
  0.0 186.1 jit_solution(2206418366028556448)
XLA Ops:
  3.8 5.3 %collective-permute-start = (bf16[320,256]{1,0:T(8,128)(2,1)S(1)}, bf16[320,256]{1,0:T(8,128)(2,1)S(1)}, u32[]{:S(2)}, u32[]{:S(2)}) collective-permute-start(bf16[320,256]{1,0:T(8,128)(2,1)S(1)} %pad_maximum_fusion.plain), channel_id=1, source_target_pairs={{0,8},{1,9},{2,10},{3,11},{4,12},{5,13},{6,14},{7,15},{8,40},{9,41... | collective-permute-start | bytes 491528 | tf_op jit(solution)/shard_map/ppermute | solution.py:55
  9.0 9.9 %collective-permute-start.1 = (bf16[320,256]{1,0:T(8,128)(2,1)S(1)}, bf16[320,256]{1,0:T(8,128)(2,1)S(1)}, u32[]{:S(2)}, u32[]{:S(2)}) collective-permute-start(bf16[320,256]{1,0:T(8,128)(2,1)S(1)} %pad_maximum_fusion.plain), channel_id=1, source_target_pairs={{0,16},{1,17},{2,18},{3,19},{4,20},{5,21},{6,22},{7,23},{8,48},{9,... | collective-permute-start | bytes 491528 | tf_op jit(solution)/shard_map/ppermute | solution.py:55
  21.2 6.9 %collective-permute-done.1.b1 = bf16[320,256]{1,0:T(8,128)(2,1)S(1)} collective-permute-done((bf16[320,256]{1,0:T(8,128)(2,1)S(1)}, bf16[320,256]{1,0:T(8,128)(2,1)S(1)}, u32[]{:S(2)}, u32[]{:S(2)}) %collective-permute-start.1) | collective-permute-done | bytes 163872 | tf_op jit(solution)/shard_map/ppermute | solution.py:55
  28.0 5.4 %collective-permute-done.2.b2 = bf16[320,256]{1,0:T(8,128)(2,1)S(1)} collective-permute-done((bf16[320,256]{1,0:T(8,128)(2,1)S(1)}, bf16[320,256]{1,0:T(8,128)(2,1)S(1)}, u32[]{:S(2)}, u32[]{:S(2)}) %collective-permute-start.2) | collective-permute-done | bytes 163872 | tf_op jit(solution)/shard_map/ppermute | solution.py:55
  38.0 6.9 %collective-permute-done.7.l1.refs_1_ = bf16[656,256]{1,0:T(8,128)(2,1)S(1)} collective-permute-done((bf16[656,256]{1,0:T(8,128)(2,1)S(1)}, bf16[656,256]{1,0:T(8,128)(2,1)S(1)}, u32[]{:S(2)}, u32[]{:S(2)}) %collective-permute-start.7) | collective-permute-done | bytes 335904 | tf_op jit(solution)/shard_map/ppermute | solution.py:70
  46.9 5.9 %collective-permute-done.9.l3.refs_3_ = bf16[656,256]{1,0:T(8,128)(2,1)S(1)} collective-permute-done((bf16[656,256]{1,0:T(8,128)(2,1)S(1)}, bf16[656,256]{1,0:T(8,128)(2,1)S(1)}, u32[]{:S(2)}, u32[]{:S(2)}) %collective-permute-start.9) | collective-permute-done | bytes 335904 | tf_op jit(solution)/shard_map/ppermute | solution.py:70
  68.6 4.4 %collective-permute-done.6.l3.refs_3_ = bf16[640,256]{1,0:T(8,128)(2,1)S(1)} collective-permute-done((bf16[640,256]{1,0:T(8,128)(2,1)S(1)}, bf16[640,256]{1,0:T(8,128)(2,1)S(1)}, u32[]{:S(2)}, u32[]{:S(2)}) %collective-permute-start.6) | collective-permute-done | bytes 327712 | tf_op jit(solution)/shard_map/ppermute | solution.py:70
  73.2 3.9 %collective-permute-done.14.p3 = bf16[448,256]{1,0:T(8,128)(2,1)S(1)} collective-permute-done((bf16[448,256]{1,0:T(8,128)(2,1)S(1)}, bf16[448,256]{1,0:T(8,128)(2,1)S(1)}, u32[]{:S(2)}, u32[]{:S(2)}) %collective-permute-start.14) | collective-permute-done | bytes 229408 | tf_op jit(solution)/shard_map/ppermute | solution.py:78
  84.5 2.7 %shard_map.128 = (bf16[432,256]{1,0:T(8,128)(2,1)S(1)}, bf16[432,256]{1,0:T(8,128)(2,1)S(1)}, bf16[432,256]{1,0:T(8,128)(2,1)S(1)}, bf16[432,256]{1,0:T(8,128)(2,1)S(1)}, bf16[1280,1024]{1,0:T(8,128)(2,1)S(1)}) custom-call(s32[4]{0:T(128)S(1)} %pad_add_fusion.pos, bf16[640,256]{1,0:T(8,128)(2,1)S(1)} %get-tuple-element.138.l0.refs_0_, ...), custom_call_target="tpu_custom_call" | custom-call | flops 1024 | bytes 1024 | tf_op jit(solution)/shard_map/pallas_call | solution.py:128
  87.2 2.6 %collective-permute-done.17.refs_6_.b2 = bf16[448,256]{1,0:T(8,128)(2,1)S(1)} collective-permute-done((bf16[448,256]{1,0:T(8,128)(2,1)S(1)}, bf16[448,256]{1,0:T(8,128)(2,1)S(1)}, u32[]{:S(2)}, u32[]{:S(2)}) %collective-permute-start.17) | collective-permute-done | bytes 229408 | tf_op jit(solution)/shard_map/ppermute | solution.py:78
  90.6 3.3 %collective-permute-start.19 = (bf16[432,256]{1,0:T(8,128)(2,1)S(1)}, bf16[432,256]{1,0:T(8,128)(2,1)S(1)}, u32[]{:S(2)}, u32[]{:S(2)}) collective-permute-start(bf16[432,256]{1,0:T(8,128)(2,1)S(1)} %get-tuple-element.151), channel_id=1, source_target_pairs={{0,64},{32,96},{64,0},{96,32},{1,65},{33,97},{65,1},{97,33},{2,66}... | collective-permute-start | bytes 663560 | tf_op jit(solution)/shard_map/ppermute | solution.py:78
  96.9 3.3 %collective-permute-done.18.one = bf16[432,256]{1,0:T(8,128)(2,1)S(1)} collective-permute-done((bf16[432,256]{1,0:T(8,128)(2,1)S(1)}, bf16[432,256]{1,0:T(8,128)(2,1)S(1)}, u32[]{:S(2)}, u32[]{:S(2)}) %collective-permute-start.18) | collective-permute-done | bytes 221216 | tf_op jit(solution)/shard_map/ppermute | solution.py:78
  100.1 3.2 %collective-permute-done.19.two = bf16[432,256]{1,0:T(8,128)(2,1)S(1)} collective-permute-done((bf16[432,256]{1,0:T(8,128)(2,1)S(1)}, bf16[432,256]{1,0:T(8,128)(2,1)S(1)}, u32[]{:S(2)}, u32[]{:S(2)}) %collective-permute-start.19) | collective-permute-done | bytes 221216 | tf_op jit(solution)/shard_map/ppermute | solution.py:78
  105.0 13.1 %collective-permute-start.22 = (bf16[448,256]{1,0:T(8,128)(2,1)S(1)}, bf16[448,256]{1,0:T(8,128)(2,1)S(1)}, u32[]{:S(2)}, u32[]{:S(2)}) collective-permute-start(bf16[448,256]{1,0:T(8,128)(2,1)S(1)} %shard_map.130.refs_0_.g0), channel_id=1, source_target_pairs={{0,64},{32,96},{64,0},{96,32},{1,65},{33,97},{65,1},{97,33},{2,66}... | collective-permute-start | bytes 688136 | tf_op jit(solution)/shard_map/ppermute | solution.py:78
  118.1 5.3 %collective-permute-done.22.refs_2_.g2 = bf16[448,256]{1,0:T(8,128)(2,1)S(1)} collective-permute-done((bf16[448,256]{1,0:T(8,128)(2,1)S(1)}, bf16[448,256]{1,0:T(8,128)(2,1)S(1)}, u32[]{:S(2)}, u32[]{:S(2)}) %collective-permute-start.22) | collective-permute-done | bytes 229408 | tf_op jit(solution)/shard_map/ppermute | solution.py:78
  123.5 4.7 %collective-permute-done.23.refs_3_.g3 = bf16[448,256]{1,0:T(8,128)(2,1)S(1)} collective-permute-done((bf16[448,256]{1,0:T(8,128)(2,1)S(1)}, bf16[448,256]{1,0:T(8,128)(2,1)S(1)}, u32[]{:S(2)}, u32[]{:S(2)}) %collective-permute-start.23) | collective-permute-done | bytes 229408 | tf_op jit(solution)/shard_map/ppermute | solution.py:78
  137.3 2.9 %collective-permute-start.31 = (bf16[4,176,256]{2,1,0:T(8,128)(2,1)S(1)}, bf16[4,176,256]{2,1,0:T(8,128)(2,1)S(1)}, u32[]{:S(2)}, u32[]{:S(2)}) collective-permute-start(bf16[4,176,256]{2,1,0:T(8,128)(2,1)S(1)} %get-tuple-element.182), channel_id=1, source_target_pairs={{0,2},{1,3},{2,4},{3,5},{4,6},{5,7},{6,0},{7,1},{8,10},{9,11},{10,... | collective-permute-start | bytes 1081352 | tf_op jit(solution)/shard_map/ppermute | solution.py:70
  141.5 3.1 %shard_map.135 = f32[432,1280]{1,0:T(8,128)} custom-call(s32[4]{0:T(128)S(1)} %pad_add_fusion.pos, bf16[432,1280]{1,0:T(8,128)(2,1)S(1)} %get-tuple-element.176.own, bf16[432,1280]{1,0:T(8,128)(2,1)S(1)} %collective-permute-done.30.other), custom_call_target="tpu_custom_call" | custom-call | flops 1024 | bytes 1024 | tf_op jit(solution)/shard_map/pallas_call | solution.py:529
  144.6 11.3 %collective-permute-done.31.one = bf16[4,176,256]{2,1,0:T(8,128)(2,1)S(1)} collective-permute-done((bf16[4,176,256]{2,1,0:T(8,128)(2,1)S(1)}, bf16[4,176,256]{2,1,0:T(8,128)(2,1)S(1)}, u32[]{:S(2)}, u32[]{:S(2)}) %collective-permute-start.31) | collective-permute-done | bytes 360480 | tf_op jit(solution)/shard_map/ppermute | solution.py:70
  155.9 3.4 %collective-permute-done.33.three = bf16[4,176,256]{2,1,0:T(8,128)(2,1)S(1)} collective-permute-done((bf16[4,176,256]{2,1,0:T(8,128)(2,1)S(1)}, bf16[4,176,256]{2,1,0:T(8,128)(2,1)S(1)}, u32[]{:S(2)}, u32[]{:S(2)}) %collective-permute-start.33) | collective-permute-done | bytes 360480 | tf_op jit(solution)/shard_map/ppermute | solution.py:70
  160.9 3.3 %collective-permute-start.35 = (bf16[176,256]{1,0:T(8,128)(2,1)S(1)}, bf16[176,256]{1,0:T(8,128)(2,1)S(1)}, u32[]{:S(2)}, u32[]{:S(2)}) collective-permute-start(bf16[176,256]{1,0:T(8,128)(2,1)S(1)} %get-tuple-element.190), channel_id=1, source_target_pairs={{0,64},{32,96},{64,0},{96,32},{1,65},{33,97},{65,1},{97,33},{2,66}... | collective-permute-start | bytes 270344 | tf_op jit(solution)/shard_map/ppermute | solution.py:78
  169.4 6.7 %collective-permute-start.38 = (bf16[176,256]{1,0:T(8,128)(2,1)S(1)}, bf16[176,256]{1,0:T(8,128)(2,1)S(1)}, u32[]{:S(2)}, u32[]{:S(2)}) collective-permute-start(bf16[176,256]{1,0:T(8,128)(2,1)S(1)} %get-tuple-element.194), channel_id=1, source_target_pairs={{0,16},{1,17},{2,18},{3,19},{4,20},{5,21},{6,22},{7,23},{8,24},{9,... | collective-permute-start | bytes 270344 | tf_op jit(solution)/shard_map/ppermute | solution.py:60
  177.4 3.1 %shard_map.138 = f32[432,1280]{1,0:T(8,128)} custom-call(s32[4]{0:T(128)S(1)} %pad_add_fusion.pos, bf16[432,1280]{1,0:T(8,128)(2,1)S(1)} %get-tuple-element.196.own, bf16[432,1280]{1,0:T(8,128)(2,1)S(1)} %collective-permute-done.40.other), custom_call_target="tpu_custom_call" | custom-call | flops 1024 | bytes 1024 | tf_op jit(solution)/shard_map/pallas_call | solution.py:529
  180.5 3.0 %collective-permute-done.38.a2 = bf16[176,256]{1,0:T(8,128)(2,1)S(1)} collective-permute-done((bf16[176,256]{1,0:T(8,128)(2,1)S(1)}, bf16[176,256]{1,0:T(8,128)(2,1)S(1)}, u32[]{:S(2)}, u32[]{:S(2)}) %collective-permute-start.38) | collective-permute-done | bytes 90144 | tf_op jit(solution)/shard_map/ppermute | solution.py:60
  (94 shorter events, 61.6 us)
Async XLA Ops:
  3.1 30.4 %collective-permute-start.3 = (bf16[336,256]{1,0:T(8,128)(2,1)S(1)}, bf16[336,256]{1,0:T(8,128)(2,1)S(1)}, u32[]{:S(2)}, u32[]{:S(2)}) collective-permute-start(bf16[336,256]{1,0:T(8,128)(2,1)S(1)} %shard_map.118), channel_id=1, source_target_pairs={{0,0},{1,1},{2,2},{3,3},{4,4},{5,5},{6,6},{7,7},{8,32},{9,33},{10,... | collective-permute-start | bytes 516104 | tf_op jit(solution)/shard_map/ppermute | solution.py:55
  3.8 17.4 %collective-permute-start = (bf16[320,256]{1,0:T(8,128)(2,1)S(1)}, bf16[320,256]{1,0:T(8,128)(2,1)S(1)}, u32[]{:S(2)}, u32[]{:S(2)}) collective-permute-start(bf16[320,256]{1,0:T(8,128)(2,1)S(1)} %pad_maximum_fusion.plain), channel_id=1, source_target_pairs={{0,8},{1,9},{2,10},{3,11},{4,12},{5,13},{6,14},{7,15},{8,40},{9,41... | collective-permute-start | bytes 491528 | tf_op jit(solution)/shard_map/ppermute | solution.py:55
  9.0 19.0 %collective-permute-start.1 = (bf16[320,256]{1,0:T(8,128)(2,1)S(1)}, bf16[320,256]{1,0:T(8,128)(2,1)S(1)}, u32[]{:S(2)}, u32[]{:S(2)}) collective-permute-start(bf16[320,256]{1,0:T(8,128)(2,1)S(1)} %pad_maximum_fusion.plain), channel_id=1, source_target_pairs={{0,16},{1,17},{2,18},{3,19},{4,20},{5,21},{6,22},{7,23},{8,48},{9,... | collective-permute-start | bytes 491528 | tf_op jit(solution)/shard_map/ppermute | solution.py:55
  18.9 14.5 %collective-permute-start.2 = (bf16[320,256]{1,0:T(8,128)(2,1)S(1)}, bf16[320,256]{1,0:T(8,128)(2,1)S(1)}, u32[]{:S(2)}, u32[]{:S(2)}) collective-permute-start(bf16[320,256]{1,0:T(8,128)(2,1)S(1)} %pad_maximum_fusion.plain), channel_id=1, source_target_pairs={{0,24},{1,25},{2,26},{3,27},{4,28},{5,29},{6,30},{7,31},{8,56},{9,... | collective-permute-start | bytes 491528 | tf_op jit(solution)/shard_map/ppermute | solution.py:55
  34.0 10.8 %collective-permute-start.7 = (bf16[656,256]{1,0:T(8,128)(2,1)S(1)}, bf16[656,256]{1,0:T(8,128)(2,1)S(1)}, u32[]{:S(2)}, u32[]{:S(2)}) collective-permute-start(bf16[656,256]{1,0:T(8,128)(2,1)S(1)} %get-tuple-element.131.l0.refs_0_), channel_id=1, source_target_pairs={{0,2},{1,3},{2,4},{3,5},{4,6},{5,7},{6,0},{7,1},{8,10},{9,11},{10,... | collective-permute-start | bytes 1007624 | tf_op jit(solution)/shard_map/ppermute | solution.py:70
  34.6 12.3 %collective-permute-start.8 = (bf16[656,256]{1,0:T(8,128)(2,1)S(1)}, bf16[656,256]{1,0:T(8,128)(2,1)S(1)}, u32[]{:S(2)}, u32[]{:S(2)}) collective-permute-start(bf16[656,256]{1,0:T(8,128)(2,1)S(1)} %get-tuple-element.131.l0.refs_0_), channel_id=1, source_target_pairs={{0,4},{1,5},{2,6},{3,7},{4,0},{5,1},{6,2},{7,3},{8,12},{9,13},{10,... | collective-permute-start | bytes 1007624 | tf_op jit(solution)/shard_map/ppermute | solution.py:70
  37.0 15.8 %collective-permute-start.9 = (bf16[656,256]{1,0:T(8,128)(2,1)S(1)}, bf16[656,256]{1,0:T(8,128)(2,1)S(1)}, u32[]{:S(2)}, u32[]{:S(2)}) collective-permute-start(bf16[656,256]{1,0:T(8,128)(2,1)S(1)} %get-tuple-element.131.l0.refs_0_), channel_id=1, source_target_pairs={{0,6},{1,7},{2,0},{3,1},{4,2},{5,3},{6,4},{7,5},{8,14},{9,15},{10,... | collective-permute-start | bytes 1007624 | tf_op jit(solution)/shard_map/ppermute | solution.py:70
  54.1 10.6 %collective-permute-start.4 = (bf16[640,256]{1,0:T(8,128)(2,1)S(1)}, bf16[640,256]{1,0:T(8,128)(2,1)S(1)}, u32[]{:S(2)}, u32[]{:S(2)}) collective-permute-start(bf16[640,256]{1,0:T(8,128)(2,1)S(1)} %get-tuple-element.138.l0.refs_0_), channel_id=1, source_target_pairs={{0,2},{1,3},{2,4},{3,5},{4,6},{5,7},{6,0},{7,1},{8,10},{9,11},{10,... | collective-permute-start | bytes 983048 | tf_op jit(solution)/shard_map/ppermute | solution.py:70
  55.0 13.5 %collective-permute-start.5 = (bf16[640,256]{1,0:T(8,128)(2,1)S(1)}, bf16[640,256]{1,0:T(8,128)(2,1)S(1)}, u32[]{:S(2)}, u32[]{:S(2)}) collective-permute-start(bf16[640,256]{1,0:T(8,128)(2,1)S(1)} %get-tuple-element.138.l0.refs_0_), channel_id=1, source_target_pairs={{0,4},{1,5},{2,6},{3,7},{4,0},{5,1},{6,2},{7,3},{8,12},{9,13},{10,... | collective-permute-start | bytes 983048 | tf_op jit(solution)/shard_map/ppermute | solution.py:70
  57.1 15.9 %collective-permute-start.6 = (bf16[640,256]{1,0:T(8,128)(2,1)S(1)}, bf16[640,256]{1,0:T(8,128)(2,1)S(1)}, u32[]{:S(2)}, u32[]{:S(2)}) collective-permute-start(bf16[640,256]{1,0:T(8,128)(2,1)S(1)} %get-tuple-element.138.l0.refs_0_), channel_id=1, source_target_pairs={{0,6},{1,7},{2,0},{3,1},{4,2},{5,3},{6,4},{7,5},{8,14},{9,15},{10,... | collective-permute-start | bytes 983048 | tf_op jit(solution)/shard_map/ppermute | solution.py:70
  59.9 13.2 %collective-permute-start.12 = (bf16[448,256]{1,0:T(8,128)(2,1)S(1)}, bf16[448,256]{1,0:T(8,128)(2,1)S(1)}, u32[]{:S(2)}, u32[]{:S(2)}) collective-permute-start(bf16[448,256]{1,0:T(8,128)(2,1)S(1)} %get-tuple-element.116), channel_id=1, source_target_pairs={{0,32},{32,64},{64,96},{96,0},{1,33},{33,65},{65,97},{97,1},{2,34}... | collective-permute-start | bytes 688136 | tf_op jit(solution)/shard_map/ppermute | solution.py:78
  64.6 12.5 %collective-permute-start.14 = (bf16[448,256]{1,0:T(8,128)(2,1)S(1)}, bf16[448,256]{1,0:T(8,128)(2,1)S(1)}, u32[]{:S(2)}, u32[]{:S(2)}) collective-permute-start(bf16[448,256]{1,0:T(8,128)(2,1)S(1)} %get-tuple-element.123), channel_id=1, source_target_pairs={{0,96},{32,0},{64,32},{96,64},{1,97},{33,1},{65,33},{97,65},{2,98}... | collective-permute-start | bytes 688136 | tf_op jit(solution)/shard_map/ppermute | solution.py:78
  81.3 12.7 %collective-permute-start.24 = (bf16[448,256]{1,0:T(8,128)(2,1)S(1)}, bf16[448,256]{1,0:T(8,128)(2,1)S(1)}, u32[]{:S(2)}, u32[]{:S(2)}) collective-permute-start(bf16[448,256]{1,0:T(8,128)(2,1)S(1)} %get-tuple-element.148.refs_4_.b0), channel_id=1, source_target_pairs={{0,32},{32,64},{64,96},{96,0},{1,33},{33,65},{65,97},{97,1},{2,34}... | collective-permute-start | bytes 688136 | tf_op jit(solution)/shard_map/ppermute | solution.py:78
  83.3 11.4 %collective-permute-start.25 = (bf16[448,256]{1,0:T(8,128)(2,1)S(1)}, bf16[448,256]{1,0:T(8,128)(2,1)S(1)}, u32[]{:S(2)}, u32[]{:S(2)}) collective-permute-start(bf16[448,256]{1,0:T(8,128)(2,1)S(1)} %get-tuple-element.148.refs_4_.b0), channel_id=1, source_target_pairs={{0,96},{32,0},{64,32},{96,64},{1,97},{33,1},{65,33},{97,65},{2,98}... | collective-permute-start | bytes 688136 | tf_op jit(solution)/shard_map/ppermute | solution.py:78
  90.6 12.7 %collective-permute-start.19 = (bf16[432,256]{1,0:T(8,128)(2,1)S(1)}, bf16[432,256]{1,0:T(8,128)(2,1)S(1)}, u32[]{:S(2)}, u32[]{:S(2)}) collective-permute-start(bf16[432,256]{1,0:T(8,128)(2,1)S(1)} %get-tuple-element.151), channel_id=1, source_target_pairs={{0,64},{32,96},{64,0},{96,32},{1,65},{33,97},{65,1},{97,33},{2,66}... | collective-permute-start | bytes 663560 | tf_op jit(solution)/shard_map/ppermute | solution.py:78
  96.8 39.6 %collective-permute-start.30 = (bf16[432,1280]{1,0:T(8,128)(2,1)S(1)}, bf16[432,1280]{1,0:T(8,128)(2,1)S(1)}, u32[]{:S(2)}, u32[]{:S(2)}) collective-permute-start(bf16[432,1280]{1,0:T(8,128)(2,1)S(1)} %get-tuple-element.176.own), channel_id=1, source_target_pairs={{0,128},{128,0},{1,129},{129,1},{2,130},{130,2},{3,131},{131,3},{4... | collective-permute-start | bytes 3317768 | tf_op jit(solution)/shard_map/ppermute | solution.py:90
  104.1 14.0 %collective-permute-start.21 = (bf16[448,256]{1,0:T(8,128)(2,1)S(1)}, bf16[448,256]{1,0:T(8,128)(2,1)S(1)}, u32[]{:S(2)}, u32[]{:S(2)}) collective-permute-start(bf16[448,256]{1,0:T(8,128)(2,1)S(1)} %shard_map.130.refs_0_.g0), channel_id=1, source_target_pairs={{0,32},{32,64},{64,96},{96,0},{1,33},{33,65},{65,97},{97,1},{2,34}... | collective-permute-start | bytes 688136 | tf_op jit(solution)/shard_map/ppermute | solution.py:78
  105.0 18.5 %collective-permute-start.22 = (bf16[448,256]{1,0:T(8,128)(2,1)S(1)}, bf16[448,256]{1,0:T(8,128)(2,1)S(1)}, u32[]{:S(2)}, u32[]{:S(2)}) collective-permute-start(bf16[448,256]{1,0:T(8,128)(2,1)S(1)} %shard_map.130.refs_0_.g0), channel_id=1, source_target_pairs={{0,64},{32,96},{64,0},{96,32},{1,65},{33,97},{65,1},{97,33},{2,66}... | collective-permute-start | bytes 688136 | tf_op jit(solution)/shard_map/ppermute | solution.py:78
  133.0 44.4 %collective-permute-start.40 = (bf16[432,1280]{1,0:T(8,128)(2,1)S(1)}, bf16[432,1280]{1,0:T(8,128)(2,1)S(1)}, u32[]{:S(2)}, u32[]{:S(2)}) collective-permute-start(bf16[432,1280]{1,0:T(8,128)(2,1)S(1)} %get-tuple-element.196.own), channel_id=1, source_target_pairs={{0,128},{128,0},{1,129},{129,1},{2,130},{130,2},{3,131},{131,3},{4... | collective-permute-start | bytes 3317768 | tf_op jit(solution)/shard_map/ppermute | solution.py:90
  137.3 18.6 %collective-permute-start.31 = (bf16[4,176,256]{2,1,0:T(8,128)(2,1)S(1)}, bf16[4,176,256]{2,1,0:T(8,128)(2,1)S(1)}, u32[]{:S(2)}, u32[]{:S(2)}) collective-permute-start(bf16[4,176,256]{2,1,0:T(8,128)(2,1)S(1)} %get-tuple-element.182), channel_id=1, source_target_pairs={{0,2},{1,3},{2,4},{3,5},{4,6},{5,7},{6,0},{7,1},{8,10},{9,11},{10,... | collective-permute-start | bytes 1081352 | tf_op jit(solution)/shard_map/ppermute | solution.py:70
  140.2 15.7 %collective-permute-start.32 = (bf16[4,176,256]{2,1,0:T(8,128)(2,1)S(1)}, bf16[4,176,256]{2,1,0:T(8,128)(2,1)S(1)}, u32[]{:S(2)}, u32[]{:S(2)}) collective-permute-start(bf16[4,176,256]{2,1,0:T(8,128)(2,1)S(1)} %get-tuple-element.183), channel_id=1, source_target_pairs={{0,4},{1,5},{2,6},{3,7},{4,0},{5,1},{6,2},{7,3},{8,12},{9,13},{10,... | collective-permute-start | bytes 1081352 | tf_op jit(solution)/shard_map/ppermute | solution.py:70
  140.4 18.8 %collective-permute-start.33 = (bf16[4,176,256]{2,1,0:T(8,128)(2,1)S(1)}, bf16[4,176,256]{2,1,0:T(8,128)(2,1)S(1)}, u32[]{:S(2)}, u32[]{:S(2)}) collective-permute-start(bf16[4,176,256]{2,1,0:T(8,128)(2,1)S(1)} %get-tuple-element.184), channel_id=1, source_target_pairs={{0,6},{1,7},{2,0},{3,1},{4,2},{5,3},{6,4},{7,5},{8,14},{9,15},{10,... | collective-permute-start | bytes 1081352 | tf_op jit(solution)/shard_map/ppermute | solution.py:70
  169.3 11.2 %collective-permute-start.37 = (bf16[176,256]{1,0:T(8,128)(2,1)S(1)}, bf16[176,256]{1,0:T(8,128)(2,1)S(1)}, u32[]{:S(2)}, u32[]{:S(2)}) collective-permute-start(bf16[176,256]{1,0:T(8,128)(2,1)S(1)} %get-tuple-element.193), channel_id=1, source_target_pairs={{0,8},{1,9},{2,10},{3,11},{4,12},{5,13},{6,14},{7,15},{8,16},{9,17... | collective-permute-start | bytes 270344 | tf_op jit(solution)/shard_map/ppermute | solution.py:60
  169.4 14.1 %collective-permute-start.38 = (bf16[176,256]{1,0:T(8,128)(2,1)S(1)}, bf16[176,256]{1,0:T(8,128)(2,1)S(1)}, u32[]{:S(2)}, u32[]{:S(2)}) collective-permute-start(bf16[176,256]{1,0:T(8,128)(2,1)S(1)} %get-tuple-element.194), channel_id=1, source_target_pairs={{0,16},{1,17},{2,18},{3,19},{4,20},{5,21},{6,22},{7,23},{8,24},{9,... | collective-permute-start | bytes 270344 | tf_op jit(solution)/shard_map/ppermute | solution.py:60
  (22 other events, 195.6 us)
where the time goes:
time: 190 us; the launch traced here: 186 us
  waiting for transfers between devices  81.5 us (43%)
  starting transfers between devices  69.7 us (37%)
  Pallas kernels  31.8 us (17%)
    ppermute x9, waiting for transfers between devices, along_x(): return lax.ppermute(values, 'col', pairs)  34.2 us
    ppermute x15, starting transfers between devices, along_row(): return lax.ppermute(values, 'row', [(a, (a + shift) % 4) for a in range(4)])  31.1 us
    ppermute x15, waiting for transfers between devices, along_row(): return lax.ppermute(values, 'row', [(a, (a + shift) % 4) for a in range(4)])  28.5 us
    pallas_call x20, Pallas kernels, run(): pl.pallas_call(kernel, in_specs=[pl.BlockSpec(memory_space=pltpu.SMEM)] +...  25.6 us
    ppermute x4, starting transfers between devices, spread_rows(): return lax.ppermute(values, ('row', 'col'), pairs)  18.1 us
    ppermute x4, waiting for transfers between devices, spread_rows(): return lax.ppermute(values, ('row', 'col'), pairs)  12.3 us
    ppermute x9, starting transfers between devices, along_x(): return lax.ppermute(values, 'col', pairs)  10.4 us
    ppermute x3, starting transfers between devices, along_high(): return lax.ppermute(values, 'col', pairs)  7.96 us
  transfers between devices with their start and end apart: 41, of which 26 were waited for; matrix products, arithmetic and copies ran while one was open for 0% of the time, Pallas kernels for 15%

commit v1 on v0

--- a/solution.py
+++ b/solution.py
@@ -538,16 +538,16 @@
     planes = whole(plane_kernel, [shaped(piece)] * 4)(
         pos, lines[0], *after([along_x(lines[p], p) for p in (1, 2, 3)], grad_second)
     )
-    planes = to_rows(planes)
+    grad_first = clips_call(own_first, other_first)
+    planes = after(to_rows(planes), grad_first)
     pieces = whole(route_kernel, [shaped(piece)] * 4, [pltpu.VMEM((4,) + piece, bf16)])(
         pos, *planes
     )
     pieces = [pieces[0]] + [along_high(pieces[p], p) for p in (1, 2, 3)]
 
-    grad_first = clips_call(own_first, other_first)
     grad_states, grad_shift, grad_scale, grad_gate = whole(
         states_kernel, [shaped(own, f32)] + [shaped((1, CHANNELS), f32)] * 3
-    )(pos, *after(pieces, grad_first), own_x, own_c, stats, scale_mod.T)
+    )(pos, *pieces, own_x, own_c, stats, scale_mod.T)
     return (
         grad_states.T[None],
         grad_first.T,

time: 190 us -> 190 us (level)
    ppermute x3, waiting for transfers between devices: 4.07 us -> 7.18 us  [along_high(): return lax.ppermute(values, 'col', pairs)]
    ppermute x15, waiting for transfers between devices: 28.5 us -> 25.4 us  [along_row(): return lax.ppermute(values, 'row', [(a, (a + shift) % 4) for a in range(4)])]
  transfers between devices with their start and end apart: 41 -> 41, of which waited for: 26 -> 25; matrix products, arithmetic and copies ran while one was open for 0% -> 0% of each run, Pallas kernels for 15% -> 15%
where the time goes in v1:
time: 190 us; the launch traced here: 186 us
  waiting for transfers between devices  81.5 us (43%)
  starting transfers between devices  69.7 us (37%)
  Pallas kernels  31.8 us (17%)
    ppermute x9, waiting for transfers between devices, along_x(): return lax.ppermute(values, 'col', pairs)  34.2 us
    ppermute x15, starting transfers between devices, along_row(): return lax.ppermute(values, 'row', [(a, (a + shift) % 4) for a in range(4)])  31.1 us
    pallas_call x20, Pallas kernels, run(): pl.pallas_call(kernel, in_specs=[pl.BlockSpec(memory_space=pltpu.SMEM)] +...  25.6 us
    ppermute x15, waiting for transfers between devices, along_row(): return lax.ppermute(values, 'row', [(a, (a + shift) % 4) for a in range(4)])  25.4 us
    ppermute x4, starting transfers between devices, spread_rows(): return lax.ppermute(values, ('row', 'col'), pairs)  18.1 us
    ppermute x4, waiting for transfers between devices, spread_rows(): return lax.ppermute(values, ('row', 'col'), pairs)  12.3 us
    ppermute x9, starting transfers between devices, along_x(): return lax.ppermute(values, 'col', pairs)  10.4 us
    ppermute x3, starting transfers between devices, along_high(): return lax.ppermute(values, 'col', pairs)  7.96 us
  transfers between devices with their start and end apart: 41, of which 25 were waited for; matrix products, arithmetic and copies ran while one was open for 0% of the time, Pallas kernels for 15%

profile of v1, /device:TPU:6, one launch (start us, length us, event | category | flops | bytes accessed | tf_op | source)
XLA Modules:
  0.0 186.1 jit_solution(14364707695741612139)
XLA Ops:
  3.8 5.3 %collective-permute-start = (bf16[320,256]{1,0:T(8,128)(2,1)S(1)}, bf16[320,256]{1,0:T(8,128)(2,1)S(1)}, u32[]{:S(2)}, u32[]{:S(2)}) collective-permute-start(bf16[320,256]{1,0:T(8,128)(2,1)S(1)} %pad_maximum_fusion.plain), channel_id=1, source_target_pairs={{0,8},{1,9},{2,10},{3,11},{4,12},{5,13},{6,14},{7,15},{8,40},{9,41... | collective-permute-start | bytes 491528 | tf_op jit(solution)/shard_map/ppermute | solution.py:55
  9.0 9.9 %collective-permute-start.1 = (bf16[320,256]{1,0:T(8,128)(2,1)S(1)}, bf16[320,256]{1,0:T(8,128)(2,1)S(1)}, u32[]{:S(2)}, u32[]{:S(2)}) collective-permute-start(bf16[320,256]{1,0:T(8,128)(2,1)S(1)} %pad_maximum_fusion.plain), channel_id=1, source_target_pairs={{0,16},{1,17},{2,18},{3,19},{4,20},{5,21},{6,22},{7,23},{8,48},{9,... | collective-permute-start | bytes 491528 | tf_op jit(solution)/shard_map/ppermute | solution.py:55
  21.2 6.9 %collective-permute-done.1.b1 = bf16[320,256]{1,0:T(8,128)(2,1)S(1)} collective-permute-done((bf16[320,256]{1,0:T(8,128)(2,1)S(1)}, bf16[320,256]{1,0:T(8,128)(2,1)S(1)}, u32[]{:S(2)}, u32[]{:S(2)}) %collective-permute-start.1) | collective-permute-done | bytes 163872 | tf_op jit(solution)/shard_map/ppermute | solution.py:55
  28.0 5.4 %collective-permute-done.2.b2 = bf16[320,256]{1,0:T(8,128)(2,1)S(1)} collective-permute-done((bf16[320,256]{1,0:T(8,128)(2,1)S(1)}, bf16[320,256]{1,0:T(8,128)(2,1)S(1)}, u32[]{:S(2)}, u32[]{:S(2)}) %collective-permute-start.2) | collective-permute-done | bytes 163872 | tf_op jit(solution)/shard_map/ppermute | solution.py:55
  38.0 6.9 %collective-permute-done.7.l1.refs_1_ = bf16[656,256]{1,0:T(8,128)(2,1)S(1)} collective-permute-done((bf16[656,256]{1,0:T(8,128)(2,1)S(1)}, bf16[656,256]{1,0:T(8,128)(2,1)S(1)}, u32[]{:S(2)}, u32[]{:S(2)}) %collective-permute-start.7) | collective-permute-done | bytes 335904 | tf_op jit(solution)/shard_map/ppermute | solution.py:70
  46.9 5.9 %collective-permute-done.9.l3.refs_3_ = bf16[656,256]{1,0:T(8,128)(2,1)S(1)} collective-permute-done((bf16[656,256]{1,0:T(8,128)(2,1)S(1)}, bf16[656,256]{1,0:T(8,128)(2,1)S(1)}, u32[]{:S(2)}, u32[]{:S(2)}) %collective-permute-start.9) | collective-permute-done | bytes 335904 | tf_op jit(solution)/shard_map/ppermute | solution.py:70
  68.6 4.4 %collective-permute-done.6.l3.refs_3_ = bf16[640,256]{1,0:T(8,128)(2,1)S(1)} collective-permute-done((bf16[640,256]{1,0:T(8,128)(2,1)S(1)}, bf16[640,256]{1,0:T(8,128)(2,1)S(1)}, u32[]{:S(2)}, u32[]{:S(2)}) %collective-permute-start.6) | collective-permute-done | bytes 327712 | tf_op jit(solution)/shard_map/ppermute | solution.py:70
  73.2 3.9 %collective-permute-done.14.p3 = bf16[448,256]{1,0:T(8,128)(2,1)S(1)} collective-permute-done((bf16[448,256]{1,0:T(8,128)(2,1)S(1)}, bf16[448,256]{1,0:T(8,128)(2,1)S(1)}, u32[]{:S(2)}, u32[]{:S(2)}) %collective-permute-start.14) | collective-permute-done | bytes 229408 | tf_op jit(solution)/shard_map/ppermute | solution.py:78
  84.5 2.7 %shard_map.128 = (bf16[432,256]{1,0:T(8,128)(2,1)S(1)}, bf16[432,256]{1,0:T(8,128)(2,1)S(1)}, bf16[432,256]{1,0:T(8,128)(2,1)S(1)}, bf16[432,256]{1,0:T(8,128)(2,1)S(1)}, bf16[1280,1024]{1,0:T(8,128)(2,1)S(1)}) custom-call(s32[4]{0:T(128)S(1)} %pad_add_fusion.pos, bf16[640,256]{1,0:T(8,128)(2,1)S(1)} %get-tuple-element.138.l0.refs_0_, ...), custom_call_target="tpu_custom_call" | custom-call | flops 1024 | bytes 1024 | tf_op jit(solution)/shard_map/pallas_call | solution.py:128
  87.2 2.6 %collective-permute-done.17.refs_6_.b2 = bf16[448,256]{1,0:T(8,128)(2,1)S(1)} collective-permute-done((bf16[448,256]{1,0:T(8,128)(2,1)S(1)}, bf16[448,256]{1,0:T(8,128)(2,1)S(1)}, u32[]{:S(2)}, u32[]{:S(2)}) %collective-permute-start.17) | collective-permute-done | bytes 229408 | tf_op jit(solution)/shard_map/ppermute | solution.py:78
  90.6 3.3 %collective-permute-start.19 = (bf16[432,256]{1,0:T(8,128)(2,1)S(1)}, bf16[432,256]{1,0:T(8,128)(2,1)S(1)}, u32[]{:S(2)}, u32[]{:S(2)}) collective-permute-start(bf16[432,256]{1,0:T(8,128)(2,1)S(1)} %get-tuple-element.151), channel_id=1, source_target_pairs={{0,64},{32,96},{64,0},{96,32},{1,65},{33,97},{65,1},{97,33},{2,66}... | collective-permute-start | bytes 663560 | tf_op jit(solution)/shard_map/ppermute | solution.py:78
  96.9 3.3 %collective-permute-done.18.one = bf16[432,256]{1,0:T(8,128)(2,1)S(1)} collective-permute-done((bf16[432,256]{1,0:T(8,128)(2,1)S(1)}, bf16[432,256]{1,0:T(8,128)(2,1)S(1)}, u32[]{:S(2)}, u32[]{:S(2)}) %collective-permute-start.18) | collective-permute-done | bytes 221216 | tf_op jit(solution)/shard_map/ppermute | solution.py:78
  100.1 3.2 %collective-permute-done.19.two = bf16[432,256]{1,0:T(8,128)(2,1)S(1)} collective-permute-done((bf16[432,256]{1,0:T(8,128)(2,1)S(1)}, bf16[432,256]{1,0:T(8,128)(2,1)S(1)}, u32[]{:S(2)}, u32[]{:S(2)}) %collective-permute-start.19) | collective-permute-done | bytes 221216 | tf_op jit(solution)/shard_map/ppermute | solution.py:78
  105.0 13.1 %collective-permute-start.22 = (bf16[448,256]{1,0:T(8,128)(2,1)S(1)}, bf16[448,256]{1,0:T(8,128)(2,1)S(1)}, u32[]{:S(2)}, u32[]{:S(2)}) collective-permute-start(bf16[448,256]{1,0:T(8,128)(2,1)S(1)} %shard_map.130.refs_0_.g0), channel_id=1, source_target_pairs={{0,64},{32,96},{64,0},{96,32},{1,65},{33,97},{65,1},{97,33},{2,66}... | collective-permute-start | bytes 688136 | tf_op jit(solution)/shard_map/ppermute | solution.py:78
  118.1 5.3 %collective-permute-done.22.refs_2_.g2 = bf16[448,256]{1,0:T(8,128)(2,1)S(1)} collective-permute-done((bf16[448,256]{1,0:T(8,128)(2,1)S(1)}, bf16[448,256]{1,0:T(8,128)(2,1)S(1)}, u32[]{:S(2)}, u32[]{:S(2)}) %collective-permute-start.22) | collective-permute-done | bytes 229408 | tf_op jit(solution)/shard_map/ppermute | solution.py:78
  123.5 4.7 %collective-permute-done.23.refs_3_.g3 = bf16[448,256]{1,0:T(8,128)(2,1)S(1)} collective-permute-done((bf16[448,256]{1,0:T(8,128)(2,1)S(1)}, bf16[448,256]{1,0:T(8,128)(2,1)S(1)}, u32[]{:S(2)}, u32[]{:S(2)}) %collective-permute-start.23) | collective-permute-done | bytes 229408 | tf_op jit(solution)/shard_map/ppermute | solution.py:78
  137.3 2.9 %collective-permute-start.31 = (bf16[4,176,256]{2,1,0:T(8,128)(2,1)S(1)}, bf16[4,176,256]{2,1,0:T(8,128)(2,1)S(1)}, u32[]{:S(2)}, u32[]{:S(2)}) collective-permute-start(bf16[4,176,256]{2,1,0:T(8,128)(2,1)S(1)} %get-tuple-element.182), channel_id=1, source_target_pairs={{0,2},{1,3},{2,4},{3,5},{4,6},{5,7},{6,0},{7,1},{8,10},{9,11},{10,... | collective-permute-start | bytes 1081352 | tf_op jit(solution)/shard_map/ppermute | solution.py:70
  141.5 3.1 %shard_map.135 = f32[432,1280]{1,0:T(8,128)} custom-call(s32[4]{0:T(128)S(1)} %pad_add_fusion.pos, bf16[432,1280]{1,0:T(8,128)(2,1)S(1)} %get-tuple-element.176.own, bf16[432,1280]{1,0:T(8,128)(2,1)S(1)} %collective-permute-done.30.other), custom_call_target="tpu_custom_call" | custom-call | flops 1024 | bytes 1024 | tf_op jit(solution)/shard_map/pallas_call | solution.py:529
  144.6 11.3 %collective-permute-done.31.one = bf16[4,176,256]{2,1,0:T(8,128)(2,1)S(1)} collective-permute-done((bf16[4,176,256]{2,1,0:T(8,128)(2,1)S(1)}, bf16[4,176,256]{2,1,0:T(8,128)(2,1)S(1)}, u32[]{:S(2)}, u32[]{:S(2)}) %collective-permute-start.31) | collective-permute-done | bytes 360480 | tf_op jit(solution)/shard_map/ppermute | solution.py:70
  155.9 3.4 %collective-permute-done.33.three = bf16[4,176,256]{2,1,0:T(8,128)(2,1)S(1)} collective-permute-done((bf16[4,176,256]{2,1,0:T(8,128)(2,1)S(1)}, bf16[4,176,256]{2,1,0:T(8,128)(2,1)S(1)}, u32[]{:S(2)}, u32[]{:S(2)}) %collective-permute-start.33) | collective-permute-done | bytes 360480 | tf_op jit(solution)/shard_map/ppermute | solution.py:70
  160.9 3.3 %collective-permute-start.35 = (bf16[176,256]{1,0:T(8,128)(2,1)S(1)}, bf16[176,256]{1,0:T(8,128)(2,1)S(1)}, u32[]{:S(2)}, u32[]{:S(2)}) collective-permute-start(bf16[176,256]{1,0:T(8,128)(2,1)S(1)} %get-tuple-element.190), channel_id=1, source_target_pairs={{0,64},{32,96},{64,0},{96,32},{1,65},{33,97},{65,1},{97,33},{2,66}... | collective-permute-start | bytes 270344 | tf_op jit(solution)/shard_map/ppermute | solution.py:78
  164.2 3.1 %shard_map.137 = f32[432,1280]{1,0:T(8,128)} custom-call(s32[4]{0:T(128)S(1)} %pad_add_fusion.pos, bf16[432,1280]{1,0:T(8,128)(2,1)S(1)} %get-tuple-element.192.own, bf16[432,1280]{1,0:T(8,128)(2,1)S(1)} %collective-permute-done.37.other), custom_call_target="tpu_custom_call" | custom-call | flops 1024 | bytes 1024 | tf_op jit(solution)/shard_map/pallas_call | solution.py:529
  169.7 6.5 %collective-permute-start.39 = (bf16[176,256]{1,0:T(8,128)(2,1)S(1)}, bf16[176,256]{1,0:T(8,128)(2,1)S(1)}, u32[]{:S(2)}, u32[]{:S(2)}) collective-permute-start(bf16[176,256]{1,0:T(8,128)(2,1)S(1)} %get-tuple-element.199), channel_id=1, source_target_pairs={{0,16},{1,17},{2,18},{3,19},{4,20},{5,21},{6,22},{7,23},{8,24},{9,... | collective-permute-start | bytes 270344 | tf_op jit(solution)/shard_map/ppermute | solution.py:60
  177.4 6.1 %collective-permute-done.39.a2 = bf16[176,256]{1,0:T(8,128)(2,1)S(1)} collective-permute-done((bf16[176,256]{1,0:T(8,128)(2,1)S(1)}, bf16[176,256]{1,0:T(8,128)(2,1)S(1)}, u32[]{:S(2)}, u32[]{:S(2)}) %collective-permute-start.39) | collective-permute-done | bytes 90144 | tf_op jit(solution)/shard_map/ppermute | solution.py:60
  (94 shorter events, 58.8 us)
Async XLA Ops:
  3.1 30.4 %collective-permute-start.3 = (bf16[336,256]{1,0:T(8,128)(2,1)S(1)}, bf16[336,256]{1,0:T(8,128)(2,1)S(1)}, u32[]{:S(2)}, u32[]{:S(2)}) collective-permute-start(bf16[336,256]{1,0:T(8,128)(2,1)S(1)} %shard_map.118), channel_id=1, source_target_pairs={{0,0},{1,1},{2,2},{3,3},{4,4},{5,5},{6,6},{7,7},{8,32},{9,33},{10,... | collective-permute-start | bytes 516104 | tf_op jit(solution)/shard_map/ppermute | solution.py:55
  3.8 17.4 %collective-permute-start = (bf16[320,256]{1,0:T(8,128)(2,1)S(1)}, bf16[320,256]{1,0:T(8,128)(2,1)S(1)}, u32[]{:S(2)}, u32[]{:S(2)}) collective-permute-start(bf16[320,256]{1,0:T(8,128)(2,1)S(1)} %pad_maximum_fusion.plain), channel_id=1, source_target_pairs={{0,8},{1,9},{2,10},{3,11},{4,12},{5,13},{6,14},{7,15},{8,40},{9,41... | collective-permute-start | bytes 491528 | tf_op jit(solution)/shard_map/ppermute | solution.py:55
  9.0 19.0 %collective-permute-start.1 = (bf16[320,256]{1,0:T(8,128)(2,1)S(1)}, bf16[320,256]{1,0:T(8,128)(2,1)S(1)}, u32[]{:S(2)}, u32[]{:S(2)}) collective-permute-start(bf16[320,256]{1,0:T(8,128)(2,1)S(1)} %pad_maximum_fusion.plain), channel_id=1, source_target_pairs={{0,16},{1,17},{2,18},{3,19},{4,20},{5,21},{6,22},{7,23},{8,48},{9,... | collective-permute-start | bytes 491528 | tf_op jit(solution)/shard_map/ppermute | solution.py:55
  18.9 14.5 %collective-permute-start.2 = (bf16[320,256]{1,0:T(8,128)(2,1)S(1)}, bf16[320,256]{1,0:T(8,128)(2,1)S(1)}, u32[]{:S(2)}, u32[]{:S(2)}) collective-permute-start(bf16[320,256]{1,0:T(8,128)(2,1)S(1)} %pad_maximum_fusion.plain), channel_id=1, source_target_pairs={{0,24},{1,25},{2,26},{3,27},{4,28},{5,29},{6,30},{7,31},{8,56},{9,... | collective-permute-start | bytes 491528 | tf_op jit(solution)/shard_map/ppermute | solution.py:55
  34.0 10.8 %collective-permute-start.7 = (bf16[656,256]{1,0:T(8,128)(2,1)S(1)}, bf16[656,256]{1,0:T(8,128)(2,1)S(1)}, u32[]{:S(2)}, u32[]{:S(2)}) collective-permute-start(bf16[656,256]{1,0:T(8,128)(2,1)S(1)} %get-tuple-element.131.l0.refs_0_), channel_id=1, source_target_pairs={{0,2},{1,3},{2,4},{3,5},{4,6},{5,7},{6,0},{7,1},{8,10},{9,11},{10,... | collective-permute-start | bytes 1007624 | tf_op jit(solution)/shard_map/ppermute | solution.py:70
  34.6 12.3 %collective-permute-start.8 = (bf16[656,256]{1,0:T(8,128)(2,1)S(1)}, bf16[656,256]{1,0:T(8,128)(2,1)S(1)}, u32[]{:S(2)}, u32[]{:S(2)}) collective-permute-start(bf16[656,256]{1,0:T(8,128)(2,1)S(1)} %get-tuple-element.131.l0.refs_0_), channel_id=1, source_target_pairs={{0,4},{1,5},{2,6},{3,7},{4,0},{5,1},{6,2},{7,3},{8,12},{9,13},{10,... | collective-permute-start | bytes 1007624 | tf_op jit(solution)/shard_map/ppermute | solution.py:70
  37.0 15.8 %collective-permute-start.9 = (bf16[656,256]{1,0:T(8,128)(2,1)S(1)}, bf16[656,256]{1,0:T(8,128)(2,1)S(1)}, u32[]{:S(2)}, u32[]{:S(2)}) collective-permute-start(bf16[656,256]{1,0:T(8,128)(2,1)S(1)} %get-tuple-element.131.l0.refs_0_), channel_id=1, source_target_pairs={{0,6},{1,7},{2,0},{3,1},{4,2},{5,3},{6,4},{7,5},{8,14},{9,15},{10,... | collective-permute-start | bytes 1007624 | tf_op jit(solution)/shard_map/ppermute | solution.py:70
  54.1 10.6 %collective-permute-start.4 = (bf16[640,256]{1,0:T(8,128)(2,1)S(1)}, bf16[640,256]{1,0:T(8,128)(2,1)S(1)}, u32[]{:S(2)}, u32[]{:S(2)}) collective-permute-start(bf16[640,256]{1,0:T(8,128)(2,1)S(1)} %get-tuple-element.138.l0.refs_0_), channel_id=1, source_target_pairs={{0,2},{1,3},{2,4},{3,5},{4,6},{5,7},{6,0},{7,1},{8,10},{9,11},{10,... | collective-permute-start | bytes 983048 | tf_op jit(solution)/shard_map/ppermute | solution.py:70
  55.0 13.5 %collective-permute-start.5 = (bf16[640,256]{1,0:T(8,128)(2,1)S(1)}, bf16[640,256]{1,0:T(8,128)(2,1)S(1)}, u32[]{:S(2)}, u32[]{:S(2)}) collective-permute-start(bf16[640,256]{1,0:T(8,128)(2,1)S(1)} %get-tuple-element.138.l0.refs_0_), channel_id=1, source_target_pairs={{0,4},{1,5},{2,6},{3,7},{4,0},{5,1},{6,2},{7,3},{8,12},{9,13},{10,... | collective-permute-start | bytes 983048 | tf_op jit(solution)/shard_map/ppermute | solution.py:70
  57.1 15.9 %collective-permute-start.6 = (bf16[640,256]{1,0:T(8,128)(2,1)S(1)}, bf16[640,256]{1,0:T(8,128)(2,1)S(1)}, u32[]{:S(2)}, u32[]{:S(2)}) collective-permute-start(bf16[640,256]{1,0:T(8,128)(2,1)S(1)} %get-tuple-element.138.l0.refs_0_), channel_id=1, source_target_pairs={{0,6},{1,7},{2,0},{3,1},{4,2},{5,3},{6,4},{7,5},{8,14},{9,15},{10,... | collective-permute-start | bytes 983048 | tf_op jit(solution)/shard_map/ppermute | solution.py:70
  59.9 13.2 %collective-permute-start.12 = (bf16[448,256]{1,0:T(8,128)(2,1)S(1)}, bf16[448,256]{1,0:T(8,128)(2,1)S(1)}, u32[]{:S(2)}, u32[]{:S(2)}) collective-permute-start(bf16[448,256]{1,0:T(8,128)(2,1)S(1)} %get-tuple-element.116), channel_id=1, source_target_pairs={{0,32},{32,64},{64,96},{96,0},{1,33},{33,65},{65,97},{97,1},{2,34}... | collective-permute-start | bytes 688136 | tf_op jit(solution)/shard_map/ppermute | solution.py:78
  64.6 12.5 %collective-permute-start.14 = (bf16[448,256]{1,0:T(8,128)(2,1)S(1)}, bf16[448,256]{1,0:T(8,128)(2,1)S(1)}, u32[]{:S(2)}, u32[]{:S(2)}) collective-permute-start(bf16[448,256]{1,0:T(8,128)(2,1)S(1)} %get-tuple-element.123), channel_id=1, source_target_pairs={{0,96},{32,0},{64,32},{96,64},{1,97},{33,1},{65,33},{97,65},{2,98}... | collective-permute-start | bytes 688136 | tf_op jit(solution)/shard_map/ppermute | solution.py:78
  81.3 12.7 %collective-permute-start.24 = (bf16[448,256]{1,0:T(8,128)(2,1)S(1)}, bf16[448,256]{1,0:T(8,128)(2,1)S(1)}, u32[]{:S(2)}, u32[]{:S(2)}) collective-permute-start(bf16[448,256]{1,0:T(8,128)(2,1)S(1)} %get-tuple-element.148.refs_4_.b0), channel_id=1, source_target_pairs={{0,32},{32,64},{64,96},{96,0},{1,33},{33,65},{65,97},{97,1},{2,34}... | collective-permute-start | bytes 688136 | tf_op jit(solution)/shard_map/ppermute | solution.py:78
  83.3 11.4 %collective-permute-start.25 = (bf16[448,256]{1,0:T(8,128)(2,1)S(1)}, bf16[448,256]{1,0:T(8,128)(2,1)S(1)}, u32[]{:S(2)}, u32[]{:S(2)}) collective-permute-start(bf16[448,256]{1,0:T(8,128)(2,1)S(1)} %get-tuple-element.148.refs_4_.b0), channel_id=1, source_target_pairs={{0,96},{32,0},{64,32},{96,64},{1,97},{33,1},{65,33},{97,65},{2,98}... | collective-permute-start | bytes 688136 | tf_op jit(solution)/shard_map/ppermute | solution.py:78
  89.8 10.3 %collective-permute-start.18 = (bf16[432,256]{1,0:T(8,128)(2,1)S(1)}, bf16[432,256]{1,0:T(8,128)(2,1)S(1)}, u32[]{:S(2)}, u32[]{:S(2)}) collective-permute-start(bf16[432,256]{1,0:T(8,128)(2,1)S(1)} %get-tuple-element.150), channel_id=1, source_target_pairs={{0,32},{32,64},{64,96},{96,0},{1,33},{33,65},{65,97},{97,1},{2,34}... | collective-permute-start | bytes 663560 | tf_op jit(solution)/shard_map/ppermute | solution.py:78
  90.6 12.7 %collective-permute-start.19 = (bf16[432,256]{1,0:T(8,128)(2,1)S(1)}, bf16[432,256]{1,0:T(8,128)(2,1)S(1)}, u32[]{:S(2)}, u32[]{:S(2)}) collective-permute-start(bf16[432,256]{1,0:T(8,128)(2,1)S(1)} %get-tuple-element.151), channel_id=1, source_target_pairs={{0,64},{32,96},{64,0},{96,32},{1,65},{33,97},{65,1},{97,33},{2,66}... | collective-permute-start | bytes 663560 | tf_op jit(solution)/shard_map/ppermute | solution.py:78
  96.8 39.6 %collective-permute-start.30 = (bf16[432,1280]{1,0:T(8,128)(2,1)S(1)}, bf16[432,1280]{1,0:T(8,128)(2,1)S(1)}, u32[]{:S(2)}, u32[]{:S(2)}) collective-permute-start(bf16[432,1280]{1,0:T(8,128)(2,1)S(1)} %get-tuple-element.176.own), channel_id=1, source_target_pairs={{0,128},{128,0},{1,129},{129,1},{2,130},{130,2},{3,131},{131,3},{4... | collective-permute-start | bytes 3317768 | tf_op jit(solution)/shard_map/ppermute | solution.py:90
  104.1 14.0 %collective-permute-start.21 = (bf16[448,256]{1,0:T(8,128)(2,1)S(1)}, bf16[448,256]{1,0:T(8,128)(2,1)S(1)}, u32[]{:S(2)}, u32[]{:S(2)}) collective-permute-start(bf16[448,256]{1,0:T(8,128)(2,1)S(1)} %shard_map.130.refs_0_.g0), channel_id=1, source_target_pairs={{0,32},{32,64},{64,96},{96,0},{1,33},{33,65},{65,97},{97,1},{2,34}... | collective-permute-start | bytes 688136 | tf_op jit(solution)/shard_map/ppermute | solution.py:78
  105.0 18.5 %collective-permute-start.22 = (bf16[448,256]{1,0:T(8,128)(2,1)S(1)}, bf16[448,256]{1,0:T(8,128)(2,1)S(1)}, u32[]{:S(2)}, u32[]{:S(2)}) collective-permute-start(bf16[448,256]{1,0:T(8,128)(2,1)S(1)} %shard_map.130.refs_0_.g0), channel_id=1, source_target_pairs={{0,64},{32,96},{64,0},{96,32},{1,65},{33,97},{65,1},{97,33},{2,66}... | collective-permute-start | bytes 688136 | tf_op jit(solution)/shard_map/ppermute | solution.py:78
  133.0 31.2 %collective-permute-start.37 = (bf16[432,1280]{1,0:T(8,128)(2,1)S(1)}, bf16[432,1280]{1,0:T(8,128)(2,1)S(1)}, u32[]{:S(2)}, u32[]{:S(2)}) collective-permute-start(bf16[432,1280]{1,0:T(8,128)(2,1)S(1)} %get-tuple-element.192.own), channel_id=1, source_target_pairs={{0,128},{128,0},{1,129},{129,1},{2,130},{130,2},{3,131},{131,3},{4... | collective-permute-start | bytes 3317768 | tf_op jit(solution)/shard_map/ppermute | solution.py:90
  137.3 18.6 %collective-permute-start.31 = (bf16[4,176,256]{2,1,0:T(8,128)(2,1)S(1)}, bf16[4,176,256]{2,1,0:T(8,128)(2,1)S(1)}, u32[]{:S(2)}, u32[]{:S(2)}) collective-permute-start(bf16[4,176,256]{2,1,0:T(8,128)(2,1)S(1)} %get-tuple-element.182), channel_id=1, source_target_pairs={{0,2},{1,3},{2,4},{3,5},{4,6},{5,7},{6,0},{7,1},{8,10},{9,11},{10,... | collective-permute-start | bytes 1081352 | tf_op jit(solution)/shard_map/ppermute | solution.py:70
  140.2 15.7 %collective-permute-start.32 = (bf16[4,176,256]{2,1,0:T(8,128)(2,1)S(1)}, bf16[4,176,256]{2,1,0:T(8,128)(2,1)S(1)}, u32[]{:S(2)}, u32[]{:S(2)}) collective-permute-start(bf16[4,176,256]{2,1,0:T(8,128)(2,1)S(1)} %get-tuple-element.183), channel_id=1, source_target_pairs={{0,4},{1,5},{2,6},{3,7},{4,0},{5,1},{6,2},{7,3},{8,12},{9,13},{10,... | collective-permute-start | bytes 1081352 | tf_op jit(solution)/shard_map/ppermute | solution.py:70
  140.4 18.8 %collective-permute-start.33 = (bf16[4,176,256]{2,1,0:T(8,128)(2,1)S(1)}, bf16[4,176,256]{2,1,0:T(8,128)(2,1)S(1)}, u32[]{:S(2)}, u32[]{:S(2)}) collective-permute-start(bf16[4,176,256]{2,1,0:T(8,128)(2,1)S(1)} %get-tuple-element.184), channel_id=1, source_target_pairs={{0,6},{1,7},{2,0},{3,1},{4,2},{5,3},{6,4},{7,5},{8,14},{9,15},{10,... | collective-permute-start | bytes 1081352 | tf_op jit(solution)/shard_map/ppermute | solution.py:70
  169.7 13.8 %collective-permute-start.39 = (bf16[176,256]{1,0:T(8,128)(2,1)S(1)}, bf16[176,256]{1,0:T(8,128)(2,1)S(1)}, u32[]{:S(2)}, u32[]{:S(2)}) collective-permute-start(bf16[176,256]{1,0:T(8,128)(2,1)S(1)} %get-tuple-element.199), channel_id=1, source_target_pairs={{0,16},{1,17},{2,18},{3,19},{4,20},{5,21},{6,22},{7,23},{8,24},{9,... | collective-permute-start | bytes 270344 | tf_op jit(solution)/shard_map/ppermute | solution.py:60
  (22 other events, 200.9 us)

commit v2 on v1

--- a/solution.py
+++ b/solution.py
@@ -502,7 +502,7 @@
         pos, *hidden, cot, mods_row, weight_two
     )
     other_second = swap_clips(own_second)
-    grad_sums = to_rows(after(grad_sums, hidden[2]))
+    grad_sums = to_rows(after(grad_sums, hidden[1]))
     (grad_pre,) = whole(grad_kernel, [shaped(wide_units)])(
         pos, *grad_sums, slope, rest, factor
     )

time: 190 us -> 191 us (level)
  the two profiles are of different devices: /device:TPU:6 before, /device:TPU:7 now
where the time goes in v2:
time: 191 us; the launch traced here: 187 us
  waiting for transfers between devices  87.1 us (46%)
  starting transfers between devices  64.8 us (34%)
  Pallas kernels  31.8 us (17%)
    ppermute x9, waiting for transfers between devices, along_x(): return lax.ppermute(values, 'col', pairs)  36 us
    ppermute x15, starting transfers between devices, along_row(): return lax.ppermute(values, 'row', [(a, (a + shift) % 4) for a in range(4)])  27.5 us
    ppermute x15, waiting for transfers between devices, along_row(): return lax.ppermute(values, 'row', [(a, (a + shift) % 4) for a in range(4)])  26.2 us
    pallas_call x20, Pallas kernels, run(): pl.pallas_call(kernel, in_specs=[pl.BlockSpec(memory_space=pltpu.SMEM)] +...  25.6 us
    ppermute x4, starting transfers between devices, spread_rows(): return lax.ppermute(values, ('row', 'col'), pairs)  17 us
    ppermute x4, waiting for transfers between devices, spread_rows(): return lax.ppermute(values, ('row', 'col'), pairs)  13.6 us
    ppermute x3, waiting for transfers between devices, along_high(): return lax.ppermute(values, 'col', pairs)  9.09 us
    ppermute x9, starting transfers between devices, along_x(): return lax.ppermute(values, 'col', pairs)  8.26 us
  transfers between devices with their start and end apart: 41, of which 25 were waited for; matrix products, arithmetic and copies ran while one was open for 0% of the time, Pallas kernels for 15%

profile of v2, /device:TPU:7, one launch (start us, length us, event | category | flops | bytes accessed | tf_op | source)
XLA Modules:
  0.0 186.8 jit_solution(9694190372110313094)
XLA Ops:
  3.8 4.7 %collective-permute-start = (bf16[320,256]{1,0:T(8,128)(2,1)S(1)}, bf16[320,256]{1,0:T(8,128)(2,1)S(1)}, u32[]{:S(2)}, u32[]{:S(2)}) collective-permute-start(bf16[320,256]{1,0:T(8,128)(2,1)S(1)} %pad_maximum_fusion.plain), channel_id=1, source_target_pairs={{0,8},{1,9},{2,10},{3,11},{4,12},{5,13},{6,14},{7,15},{8,40},{9,41... | collective-permute-start | bytes 491528 | tf_op jit(solution)/shard_map/ppermute | solution.py:55
  8.5 9.6 %collective-permute-start.1 = (bf16[320,256]{1,0:T(8,128)(2,1)S(1)}, bf16[320,256]{1,0:T(8,128)(2,1)S(1)}, u32[]{:S(2)}, u32[]{:S(2)}) collective-permute-start(bf16[320,256]{1,0:T(8,128)(2,1)S(1)} %pad_maximum_fusion.plain), channel_id=1, source_target_pairs={{0,16},{1,17},{2,18},{3,19},{4,20},{5,21},{6,22},{7,23},{8,48},{9,... | collective-permute-start | bytes 491528 | tf_op jit(solution)/shard_map/ppermute | solution.py:55
  20.2 6.9 %collective-permute-done.1.b1 = bf16[320,256]{1,0:T(8,128)(2,1)S(1)} collective-permute-done((bf16[320,256]{1,0:T(8,128)(2,1)S(1)}, bf16[320,256]{1,0:T(8,128)(2,1)S(1)}, u32[]{:S(2)}, u32[]{:S(2)}) %collective-permute-start.1) | collective-permute-done | bytes 163872 | tf_op jit(solution)/shard_map/ppermute | solution.py:55
  27.1 6.5 %collective-permute-done.2.b2 = bf16[320,256]{1,0:T(8,128)(2,1)S(1)} collective-permute-done((bf16[320,256]{1,0:T(8,128)(2,1)S(1)}, bf16[320,256]{1,0:T(8,128)(2,1)S(1)}, u32[]{:S(2)}, u32[]{:S(2)}) %collective-permute-start.2) | collective-permute-done | bytes 163872 | tf_op jit(solution)/shard_map/ppermute | solution.py:55
  37.6 5.7 %collective-permute-done.7.l1.refs_1_ = bf16[656,256]{1,0:T(8,128)(2,1)S(1)} collective-permute-done((bf16[656,256]{1,0:T(8,128)(2,1)S(1)}, bf16[656,256]{1,0:T(8,128)(2,1)S(1)}, u32[]{:S(2)}, u32[]{:S(2)}) %collective-permute-start.7) | collective-permute-done | bytes 335904 | tf_op jit(solution)/shard_map/ppermute | solution.py:70
  44.7 8.3 %collective-permute-done.9.l3.refs_3_ = bf16[656,256]{1,0:T(8,128)(2,1)S(1)} collective-permute-done((bf16[656,256]{1,0:T(8,128)(2,1)S(1)}, bf16[656,256]{1,0:T(8,128)(2,1)S(1)}, u32[]{:S(2)}, u32[]{:S(2)}) %collective-permute-start.9) | collective-permute-done | bytes 335904 | tf_op jit(solution)/shard_map/ppermute | solution.py:70
  67.7 5.5 %collective-permute-done.6.l3.refs_3_ = bf16[640,256]{1,0:T(8,128)(2,1)S(1)} collective-permute-done((bf16[640,256]{1,0:T(8,128)(2,1)S(1)}, bf16[640,256]{1,0:T(8,128)(2,1)S(1)}, u32[]{:S(2)}, u32[]{:S(2)}) %collective-permute-start.6) | collective-permute-done | bytes 327712 | tf_op jit(solution)/shard_map/ppermute | solution.py:70
  73.2 3.0 %collective-permute-done.14.p3 = bf16[448,256]{1,0:T(8,128)(2,1)S(1)} collective-permute-done((bf16[448,256]{1,0:T(8,128)(2,1)S(1)}, bf16[448,256]{1,0:T(8,128)(2,1)S(1)}, u32[]{:S(2)}, u32[]{:S(2)}) %collective-permute-start.14) | collective-permute-done | bytes 229408 | tf_op jit(solution)/shard_map/ppermute | solution.py:78
  80.6 3.0 %collective-permute-start.24 = (bf16[448,256]{1,0:T(8,128)(2,1)S(1)}, bf16[448,256]{1,0:T(8,128)(2,1)S(1)}, u32[]{:S(2)}, u32[]{:S(2)}) collective-permute-start(bf16[448,256]{1,0:T(8,128)(2,1)S(1)} %get-tuple-element.148.refs_4_.b0), channel_id=1, source_target_pairs={{0,64},{32,96},{64,0},{96,32},{1,65},{33,97},{65,1},{97,33},{2,66}... | collective-permute-start | bytes 688136 | tf_op jit(solution)/shard_map/ppermute | solution.py:78
  83.6 2.7 %shard_map.128 = (bf16[432,256]{1,0:T(8,128)(2,1)S(1)}, bf16[432,256]{1,0:T(8,128)(2,1)S(1)}, bf16[432,256]{1,0:T(8,128)(2,1)S(1)}, bf16[432,256]{1,0:T(8,128)(2,1)S(1)}, bf16[1280,1024]{1,0:T(8,128)(2,1)S(1)}) custom-call(s32[4]{0:T(128)S(1)} %pad_add_fusion.pos, bf16[640,256]{1,0:T(8,128)(2,1)S(1)} %get-tuple-element.138.l0.refs_0_, ...), custom_call_target="tpu_custom_call" | custom-call | flops 1024 | bytes 1024 | tf_op jit(solution)/shard_map/pallas_call | solution.py:128
  90.7 3.1 %collective-permute-done.24.refs_6_.b2 = bf16[448,256]{1,0:T(8,128)(2,1)S(1)} collective-permute-done((bf16[448,256]{1,0:T(8,128)(2,1)S(1)}, bf16[448,256]{1,0:T(8,128)(2,1)S(1)}, u32[]{:S(2)}, u32[]{:S(2)}) %collective-permute-start.24) | collective-permute-done | bytes 229408 | tf_op jit(solution)/shard_map/ppermute | solution.py:78
  96.1 3.9 %collective-permute-done.18.one = bf16[432,256]{1,0:T(8,128)(2,1)S(1)} collective-permute-done((bf16[432,256]{1,0:T(8,128)(2,1)S(1)}, bf16[432,256]{1,0:T(8,128)(2,1)S(1)}, u32[]{:S(2)}, u32[]{:S(2)}) %collective-permute-start.18) | collective-permute-done | bytes 221216 | tf_op jit(solution)/shard_map/ppermute | solution.py:78
  100.0 3.3 %collective-permute-done.19.two = bf16[432,256]{1,0:T(8,128)(2,1)S(1)} collective-permute-done((bf16[432,256]{1,0:T(8,128)(2,1)S(1)}, bf16[432,256]{1,0:T(8,128)(2,1)S(1)}, u32[]{:S(2)}, u32[]{:S(2)}) %collective-permute-start.19) | collective-permute-done | bytes 221216 | tf_op jit(solution)/shard_map/ppermute | solution.py:78
  105.1 12.9 %collective-permute-start.22 = (bf16[448,256]{1,0:T(8,128)(2,1)S(1)}, bf16[448,256]{1,0:T(8,128)(2,1)S(1)}, u32[]{:S(2)}, u32[]{:S(2)}) collective-permute-start(bf16[448,256]{1,0:T(8,128)(2,1)S(1)} %shard_map.130.refs_0_.g0), channel_id=1, source_target_pairs={{0,64},{32,96},{64,0},{96,32},{1,65},{33,97},{65,1},{97,33},{2,66}... | collective-permute-start | bytes 688136 | tf_op jit(solution)/shard_map/ppermute | solution.py:78
  118.0 4.9 %collective-permute-done.22.refs_2_.g2 = bf16[448,256]{1,0:T(8,128)(2,1)S(1)} collective-permute-done((bf16[448,256]{1,0:T(8,128)(2,1)S(1)}, bf16[448,256]{1,0:T(8,128)(2,1)S(1)}, u32[]{:S(2)}, u32[]{:S(2)}) %collective-permute-start.22) | collective-permute-done | bytes 229408 | tf_op jit(solution)/shard_map/ppermute | solution.py:78
  122.9 4.8 %collective-permute-done.23.refs_3_.g3 = bf16[448,256]{1,0:T(8,128)(2,1)S(1)} collective-permute-done((bf16[448,256]{1,0:T(8,128)(2,1)S(1)}, bf16[448,256]{1,0:T(8,128)(2,1)S(1)}, u32[]{:S(2)}, u32[]{:S(2)}) %collective-permute-start.23) | collective-permute-done | bytes 229408 | tf_op jit(solution)/shard_map/ppermute | solution.py:78
  141.4 3.1 %shard_map.135 = f32[432,1280]{1,0:T(8,128)} custom-call(s32[4]{0:T(128)S(1)} %pad_add_fusion.pos, bf16[432,1280]{1,0:T(8,128)(2,1)S(1)} %get-tuple-element.176.own, bf16[432,1280]{1,0:T(8,128)(2,1)S(1)} %collective-permute-done.30.other), custom_call_target="tpu_custom_call" | custom-call | flops 1024 | bytes 1024 | tf_op jit(solution)/shard_map/pallas_call | solution.py:529
  144.5 11.2 %collective-permute-done.31.one = bf16[4,176,256]{2,1,0:T(8,128)(2,1)S(1)} collective-permute-done((bf16[4,176,256]{2,1,0:T(8,128)(2,1)S(1)}, bf16[4,176,256]{2,1,0:T(8,128)(2,1)S(1)}, u32[]{:S(2)}, u32[]{:S(2)}) %collective-permute-start.31) | collective-permute-done | bytes 360480 | tf_op jit(solution)/shard_map/ppermute | solution.py:70
  155.6 3.9 %collective-permute-done.33.three = bf16[4,176,256]{2,1,0:T(8,128)(2,1)S(1)} collective-permute-done((bf16[4,176,256]{2,1,0:T(8,128)(2,1)S(1)}, bf16[4,176,256]{2,1,0:T(8,128)(2,1)S(1)}, u32[]{:S(2)}, u32[]{:S(2)}) %collective-permute-start.33) | collective-permute-done | bytes 360480 | tf_op jit(solution)/shard_map/ppermute | solution.py:70
  160.8 3.1 %collective-permute-start.35 = (bf16[176,256]{1,0:T(8,128)(2,1)S(1)}, bf16[176,256]{1,0:T(8,128)(2,1)S(1)}, u32[]{:S(2)}, u32[]{:S(2)}) collective-permute-start(bf16[176,256]{1,0:T(8,128)(2,1)S(1)} %get-tuple-element.190), channel_id=1, source_target_pairs={{0,64},{32,96},{64,0},{96,32},{1,65},{33,97},{65,1},{97,33},{2,66}... | collective-permute-start | bytes 270344 | tf_op jit(solution)/shard_map/ppermute | solution.py:78
  163.9 3.1 %shard_map.137 = f32[432,1280]{1,0:T(8,128)} custom-call(s32[4]{0:T(128)S(1)} %pad_add_fusion.pos, bf16[432,1280]{1,0:T(8,128)(2,1)S(1)} %get-tuple-element.192.own, bf16[432,1280]{1,0:T(8,128)(2,1)S(1)} %collective-permute-done.37.other), custom_call_target="tpu_custom_call" | custom-call | flops 1024 | bytes 1024 | tf_op jit(solution)/shard_map/pallas_call | solution.py:529
  169.1 6.4 %collective-permute-start.39 = (bf16[176,256]{1,0:T(8,128)(2,1)S(1)}, bf16[176,256]{1,0:T(8,128)(2,1)S(1)}, u32[]{:S(2)}, u32[]{:S(2)}) collective-permute-start(bf16[176,256]{1,0:T(8,128)(2,1)S(1)} %get-tuple-element.199), channel_id=1, source_target_pairs={{0,16},{1,17},{2,18},{3,19},{4,20},{5,21},{6,22},{7,23},{8,24},{9,... | collective-permute-start | bytes 270344 | tf_op jit(solution)/shard_map/ppermute | solution.py:60
  176.2 5.3 %collective-permute-done.39.a2 = bf16[176,256]{1,0:T(8,128)(2,1)S(1)} collective-permute-done((bf16[176,256]{1,0:T(8,128)(2,1)S(1)}, bf16[176,256]{1,0:T(8,128)(2,1)S(1)}, u32[]{:S(2)}, u32[]{:S(2)}) %collective-permute-start.39) | collective-permute-done | bytes 90144 | tf_op jit(solution)/shard_map/ppermute | solution.py:60
  181.5 3.8 %collective-permute-done.40.a3 = bf16[176,256]{1,0:T(8,128)(2,1)S(1)} collective-permute-done((bf16[176,256]{1,0:T(8,128)(2,1)S(1)}, bf16[176,256]{1,0:T(8,128)(2,1)S(1)}, u32[]{:S(2)}, u32[]{:S(2)}) %collective-permute-start.40) | collective-permute-done | bytes 90144 | tf_op jit(solution)/shard_map/ppermute | solution.py:60
  (94 shorter events, 57.0 us)
Async XLA Ops:
  3.1 30.6 %collective-permute-start.3 = (bf16[336,256]{1,0:T(8,128)(2,1)S(1)}, bf16[336,256]{1,0:T(8,128)(2,1)S(1)}, u32[]{:S(2)}, u32[]{:S(2)}) collective-permute-start(bf16[336,256]{1,0:T(8,128)(2,1)S(1)} %shard_map.118), channel_id=1, source_target_pairs={{0,0},{1,1},{2,2},{3,3},{4,4},{5,5},{6,6},{7,7},{8,32},{9,33},{10,... | collective-permute-start | bytes 516104 | tf_op jit(solution)/shard_map/ppermute | solution.py:55
  3.8 16.4 %collective-permute-start = (bf16[320,256]{1,0:T(8,128)(2,1)S(1)}, bf16[320,256]{1,0:T(8,128)(2,1)S(1)}, u32[]{:S(2)}, u32[]{:S(2)}) collective-permute-start(bf16[320,256]{1,0:T(8,128)(2,1)S(1)} %pad_maximum_fusion.plain), channel_id=1, source_target_pairs={{0,8},{1,9},{2,10},{3,11},{4,12},{5,13},{6,14},{7,15},{8,40},{9,41... | collective-permute-start | bytes 491528 | tf_op jit(solution)/shard_map/ppermute | solution.py:55
  8.5 18.7 %collective-permute-start.1 = (bf16[320,256]{1,0:T(8,128)(2,1)S(1)}, bf16[320,256]{1,0:T(8,128)(2,1)S(1)}, u32[]{:S(2)}, u32[]{:S(2)}) collective-permute-start(bf16[320,256]{1,0:T(8,128)(2,1)S(1)} %pad_maximum_fusion.plain), channel_id=1, source_target_pairs={{0,16},{1,17},{2,18},{3,19},{4,20},{5,21},{6,22},{7,23},{8,48},{9,... | collective-permute-start | bytes 491528 | tf_op jit(solution)/shard_map/ppermute | solution.py:55
  18.1 15.6 %collective-permute-start.2 = (bf16[320,256]{1,0:T(8,128)(2,1)S(1)}, bf16[320,256]{1,0:T(8,128)(2,1)S(1)}, u32[]{:S(2)}, u32[]{:S(2)}) collective-permute-start(bf16[320,256]{1,0:T(8,128)(2,1)S(1)} %pad_maximum_fusion.plain), channel_id=1, source_target_pairs={{0,24},{1,25},{2,26},{3,27},{4,28},{5,29},{6,30},{7,31},{8,56},{9,... | collective-permute-start | bytes 491528 | tf_op jit(solution)/shard_map/ppermute | solution.py:55
  34.5 10.2 %collective-permute-start.8 = (bf16[656,256]{1,0:T(8,128)(2,1)S(1)}, bf16[656,256]{1,0:T(8,128)(2,1)S(1)}, u32[]{:S(2)}, u32[]{:S(2)}) collective-permute-start(bf16[656,256]{1,0:T(8,128)(2,1)S(1)} %get-tuple-element.131.l0.refs_0_), channel_id=1, source_target_pairs={{0,4},{1,5},{2,6},{3,7},{4,0},{5,1},{6,2},{7,3},{8,12},{9,13},{10,... | collective-permute-start | bytes 1007624 | tf_op jit(solution)/shard_map/ppermute | solution.py:70
  36.6 16.4 %collective-permute-start.9 = (bf16[656,256]{1,0:T(8,128)(2,1)S(1)}, bf16[656,256]{1,0:T(8,128)(2,1)S(1)}, u32[]{:S(2)}, u32[]{:S(2)}) collective-permute-start(bf16[656,256]{1,0:T(8,128)(2,1)S(1)} %get-tuple-element.131.l0.refs_0_), channel_id=1, source_target_pairs={{0,6},{1,7},{2,0},{3,1},{4,2},{5,3},{6,4},{7,5},{8,14},{9,15},{10,... | collective-permute-start | bytes 1007624 | tf_op jit(solution)/shard_map/ppermute | solution.py:70
  55.0 12.7 %collective-permute-start.5 = (bf16[640,256]{1,0:T(8,128)(2,1)S(1)}, bf16[640,256]{1,0:T(8,128)(2,1)S(1)}, u32[]{:S(2)}, u32[]{:S(2)}) collective-permute-start(bf16[640,256]{1,0:T(8,128)(2,1)S(1)} %get-tuple-element.138.l0.refs_0_), channel_id=1, source_target_pairs={{0,4},{1,5},{2,6},{3,7},{4,0},{5,1},{6,2},{7,3},{8,12},{9,13},{10,... | collective-permute-start | bytes 983048 | tf_op jit(solution)/shard_map/ppermute | solution.py:70
  56.8 16.4 %collective-permute-start.6 = (bf16[640,256]{1,0:T(8,128)(2,1)S(1)}, bf16[640,256]{1,0:T(8,128)(2,1)S(1)}, u32[]{:S(2)}, u32[]{:S(2)}) collective-permute-start(bf16[640,256]{1,0:T(8,128)(2,1)S(1)} %get-tuple-element.138.l0.refs_0_), channel_id=1, source_target_pairs={{0,6},{1,7},{2,0},{3,1},{4,2},{5,3},{6,4},{7,5},{8,14},{9,15},{10,... | collective-permute-start | bytes 983048 | tf_op jit(solution)/shard_map/ppermute | solution.py:70
  59.6 13.5 %collective-permute-start.12 = (bf16[448,256]{1,0:T(8,128)(2,1)S(1)}, bf16[448,256]{1,0:T(8,128)(2,1)S(1)}, u32[]{:S(2)}, u32[]{:S(2)}) collective-permute-start(bf16[448,256]{1,0:T(8,128)(2,1)S(1)} %get-tuple-element.116), channel_id=1, source_target_pairs={{0,32},{32,64},{64,96},{96,0},{1,33},{33,65},{65,97},{97,1},{2,34}... | collective-permute-start | bytes 688136 | tf_op jit(solution)/shard_map/ppermute | solution.py:78
  63.9 12.3 %collective-permute-start.14 = (bf16[448,256]{1,0:T(8,128)(2,1)S(1)}, bf16[448,256]{1,0:T(8,128)(2,1)S(1)}, u32[]{:S(2)}, u32[]{:S(2)}) collective-permute-start(bf16[448,256]{1,0:T(8,128)(2,1)S(1)} %get-tuple-element.123), channel_id=1, source_target_pairs={{0,96},{32,0},{64,32},{96,64},{1,97},{33,1},{65,33},{97,65},{2,98}... | collective-permute-start | bytes 688136 | tf_op jit(solution)/shard_map/ppermute | solution.py:78
  80.6 13.3 %collective-permute-start.24 = (bf16[448,256]{1,0:T(8,128)(2,1)S(1)}, bf16[448,256]{1,0:T(8,128)(2,1)S(1)}, u32[]{:S(2)}, u32[]{:S(2)}) collective-permute-start(bf16[448,256]{1,0:T(8,128)(2,1)S(1)} %get-tuple-element.148.refs_4_.b0), channel_id=1, source_target_pairs={{0,64},{32,96},{64,0},{96,32},{1,65},{33,97},{65,1},{97,33},{2,66}... | collective-permute-start | bytes 688136 | tf_op jit(solution)/shard_map/ppermute | solution.py:78
  83.6 10.3 %collective-permute-start.25 = (bf16[448,256]{1,0:T(8,128)(2,1)S(1)}, bf16[448,256]{1,0:T(8,128)(2,1)S(1)}, u32[]{:S(2)}, u32[]{:S(2)}) collective-permute-start(bf16[448,256]{1,0:T(8,128)(2,1)S(1)} %get-tuple-element.148.refs_4_.b0), channel_id=1, source_target_pairs={{0,96},{32,0},{64,32},{96,64},{1,97},{33,1},{65,33},{97,65},{2,98}... | collective-permute-start | bytes 688136 | tf_op jit(solution)/shard_map/ppermute | solution.py:78
  88.0 12.0 %collective-permute-start.18 = (bf16[432,256]{1,0:T(8,128)(2,1)S(1)}, bf16[432,256]{1,0:T(8,128)(2,1)S(1)}, u32[]{:S(2)}, u32[]{:S(2)}) collective-permute-start(bf16[432,256]{1,0:T(8,128)(2,1)S(1)} %get-tuple-element.150), channel_id=1, source_target_pairs={{0,32},{32,64},{64,96},{96,0},{1,33},{33,65},{65,97},{97,1},{2,34}... | collective-permute-start | bytes 663560 | tf_op jit(solution)/shard_map/ppermute | solution.py:78
  88.0 15.3 %collective-permute-start.19 = (bf16[432,256]{1,0:T(8,128)(2,1)S(1)}, bf16[432,256]{1,0:T(8,128)(2,1)S(1)}, u32[]{:S(2)}, u32[]{:S(2)}) collective-permute-start(bf16[432,256]{1,0:T(8,128)(2,1)S(1)} %get-tuple-element.151), channel_id=1, source_target_pairs={{0,64},{32,96},{64,0},{96,32},{1,65},{33,97},{65,1},{97,33},{2,66}... | collective-permute-start | bytes 663560 | tf_op jit(solution)/shard_map/ppermute | solution.py:78
  90.4 13.0 %collective-permute-start.20 = (bf16[432,256]{1,0:T(8,128)(2,1)S(1)}, bf16[432,256]{1,0:T(8,128)(2,1)S(1)}, u32[]{:S(2)}, u32[]{:S(2)}) collective-permute-start(bf16[432,256]{1,0:T(8,128)(2,1)S(1)} %get-tuple-element.152), channel_id=1, source_target_pairs={{0,96},{32,0},{64,32},{96,64},{1,97},{33,1},{65,33},{97,65},{2,98}... | collective-permute-start | bytes 663560 | tf_op jit(solution)/shard_map/ppermute | solution.py:78
  96.0 41.2 %collective-permute-start.30 = (bf16[432,1280]{1,0:T(8,128)(2,1)S(1)}, bf16[432,1280]{1,0:T(8,128)(2,1)S(1)}, u32[]{:S(2)}, u32[]{:S(2)}) collective-permute-start(bf16[432,1280]{1,0:T(8,128)(2,1)S(1)} %get-tuple-element.176.own), channel_id=1, source_target_pairs={{0,128},{128,0},{1,129},{129,1},{2,130},{130,2},{3,131},{131,3},{4... | collective-permute-start | bytes 3317768 | tf_op jit(solution)/shard_map/ppermute | solution.py:90
  104.1 13.9 %collective-permute-start.21 = (bf16[448,256]{1,0:T(8,128)(2,1)S(1)}, bf16[448,256]{1,0:T(8,128)(2,1)S(1)}, u32[]{:S(2)}, u32[]{:S(2)}) collective-permute-start(bf16[448,256]{1,0:T(8,128)(2,1)S(1)} %shard_map.130.refs_0_.g0), channel_id=1, source_target_pairs={{0,32},{32,64},{64,96},{96,0},{1,33},{33,65},{65,97},{97,1},{2,34}... | collective-permute-start | bytes 688136 | tf_op jit(solution)/shard_map/ppermute | solution.py:78
  105.1 17.8 %collective-permute-start.22 = (bf16[448,256]{1,0:T(8,128)(2,1)S(1)}, bf16[448,256]{1,0:T(8,128)(2,1)S(1)}, u32[]{:S(2)}, u32[]{:S(2)}) collective-permute-start(bf16[448,256]{1,0:T(8,128)(2,1)S(1)} %shard_map.130.refs_0_.g0), channel_id=1, source_target_pairs={{0,64},{32,96},{64,0},{96,32},{1,65},{33,97},{65,1},{97,33},{2,66}... | collective-permute-start | bytes 688136 | tf_op jit(solution)/shard_map/ppermute | solution.py:78
  134.1 29.8 %collective-permute-start.37 = (bf16[432,1280]{1,0:T(8,128)(2,1)S(1)}, bf16[432,1280]{1,0:T(8,128)(2,1)S(1)}, u32[]{:S(2)}, u32[]{:S(2)}) collective-permute-start(bf16[432,1280]{1,0:T(8,128)(2,1)S(1)} %get-tuple-element.192.own), channel_id=1, source_target_pairs={{0,128},{128,0},{1,129},{129,1},{2,130},{130,2},{3,131},{131,3},{4... | collective-permute-start | bytes 3317768 | tf_op jit(solution)/shard_map/ppermute | solution.py:90
  138.0 17.6 %collective-permute-start.31 = (bf16[4,176,256]{2,1,0:T(8,128)(2,1)S(1)}, bf16[4,176,256]{2,1,0:T(8,128)(2,1)S(1)}, u32[]{:S(2)}, u32[]{:S(2)}) collective-permute-start(bf16[4,176,256]{2,1,0:T(8,128)(2,1)S(1)} %get-tuple-element.182), channel_id=1, source_target_pairs={{0,2},{1,3},{2,4},{3,5},{4,6},{5,7},{6,0},{7,1},{8,10},{9,11},{10,... | collective-permute-start | bytes 1081352 | tf_op jit(solution)/shard_map/ppermute | solution.py:70
  140.6 15.0 %collective-permute-start.32 = (bf16[4,176,256]{2,1,0:T(8,128)(2,1)S(1)}, bf16[4,176,256]{2,1,0:T(8,128)(2,1)S(1)}, u32[]{:S(2)}, u32[]{:S(2)}) collective-permute-start(bf16[4,176,256]{2,1,0:T(8,128)(2,1)S(1)} %get-tuple-element.183), channel_id=1, source_target_pairs={{0,4},{1,5},{2,6},{3,7},{4,0},{5,1},{6,2},{7,3},{8,12},{9,13},{10,... | collective-permute-start | bytes 1081352 | tf_op jit(solution)/shard_map/ppermute | solution.py:70
  140.6 18.9 %collective-permute-start.33 = (bf16[4,176,256]{2,1,0:T(8,128)(2,1)S(1)}, bf16[4,176,256]{2,1,0:T(8,128)(2,1)S(1)}, u32[]{:S(2)}, u32[]{:S(2)}) collective-permute-start(bf16[4,176,256]{2,1,0:T(8,128)(2,1)S(1)} %get-tuple-element.184), channel_id=1, source_target_pairs={{0,6},{1,7},{2,0},{3,1},{4,2},{5,3},{6,4},{7,5},{8,14},{9,15},{10,... | collective-permute-start | bytes 1081352 | tf_op jit(solution)/shard_map/ppermute | solution.py:70
  169.1 12.5 %collective-permute-start.39 = (bf16[176,256]{1,0:T(8,128)(2,1)S(1)}, bf16[176,256]{1,0:T(8,128)(2,1)S(1)}, u32[]{:S(2)}, u32[]{:S(2)}) collective-permute-start(bf16[176,256]{1,0:T(8,128)(2,1)S(1)} %get-tuple-element.199), channel_id=1, source_target_pairs={{0,16},{1,17},{2,18},{3,19},{4,20},{5,21},{6,22},{7,23},{8,24},{9,... | collective-permute-start | bytes 270344 | tf_op jit(solution)/shard_map/ppermute | solution.py:60
  175.4 9.9 %collective-permute-start.40 = (bf16[176,256]{1,0:T(8,128)(2,1)S(1)}, bf16[176,256]{1,0:T(8,128)(2,1)S(1)}, u32[]{:S(2)}, u32[]{:S(2)}) collective-permute-start(bf16[176,256]{1,0:T(8,128)(2,1)S(1)} %get-tuple-element.200), channel_id=1, source_target_pairs={{0,24},{1,25},{2,26},{3,27},{4,28},{5,29},{6,30},{7,31},{8,0},{9,1... | collective-permute-start | bytes 270344 | tf_op jit(solution)/shard_map/ppermute | solution.py:60
  (22 other events, 195.8 us)
